TPU v7x, 256 devices: a whole 4x4x8 slice. The times are simulated.
256 devices in a mesh: member: 8 (over x, core), space: 32 (over z, y).
Axes of the slice: x: 4, y: 4, z: 8, core: 2. Of those that a mesh axis runs over, the one named last changes fastest.
Arguments:
- inputs: bfloat16 [32, 512, 32768], P('member', None, 'space'), may hold values from -6 to 6
- w_in: bfloat16 [512, 512], P('space'), may hold values from -0.25 to 0.25
- bias_in: float32 [512], replicated, may hold values from -3 to 3
- w_out: bfloat16 [512, 87], P('space'), may hold values from -0.25 to 0.25
- members_out: float32 [32, 87, 32768], P('member', None, 'space'), may hold values from 0 to 16, as said below
- target: float32 [87, 32768], P(None, 'space'), may hold values from 0 to 16, as said below
- cell_area: float32 [32768], P('space'), may hold values from 0.5 to 1.5
Outputs:
- input_grad: bfloat16 [32, 512, 32768], P('member', None, 'space')
- w_in_grad: float32 [512, 512], P('space')
- w_out_grad: float32 [512, 87], P('space')
- bias_grad: float32 [512], P('space')
Inputs may be any that keep to these rules, and one draw needn't show every extreme that they name: `members_out`: every value is an integer multiple of 2^-18; at each channel and cell the 32 members hold distinct values. `target`: every value is an odd multiple of 2^-19, so it never equals a member's value.
All inputs are finite; a program needn't handle non-finite values.
Results may differ from a plain program's by a relative error of at most 0.024.
Values may be sent and summed in bfloat16 or wider, within the bound.
A program may use at most 128 MiB of HBM per device.

v0:
```python
import math

import jax
import jax.numpy as jnp
from jax import lax
from jax.sharding import PartitionSpec as P

cubic_coef = 0.044715
root_coef = 0.7978845608028654


def gelu_parts(values):
    inner = root_coef * (values + cubic_coef * values * values * values)
    curve = jnp.tanh(inner)
    activated = 0.5 * values * (1.0 + curve)
    slope = 0.5 * (1.0 + curve) + 0.5 * values * (1.0 - curve * curve) * root_coef * (
        1.0 + 3.0 * cubic_coef * values * values
    )
    return (activated, slope)


def body(inputs, w_in, bias_in, w_out, members_out, target, cell_area):
    w_in_all, w_out_all = (
        lax.all_gather(w_in, "space", axis=0, tiled=True),
        lax.all_gather(w_out, "space", axis=0, tiled=True),
    )
    own_members = members_out.shape[0]
    member_size = lax.axis_size("member")
    space_size = lax.axis_size("space")
    member_count = own_members * member_size
    cell_count = cell_area.shape[0] * space_size
    target_sign = jnp.sign(members_out - target[None])
    gathered = lax.all_to_all(members_out, "member", split_axis=2, concat_axis=0, tiled=True)
    sums = jnp.zeros(gathered.shape, jnp.float32)
    for offset in range(0, member_count, 8):
        ending = min(offset + 8, member_count)
        sums = sums + jnp.sum(jnp.sign(gathered[:, None] - gathered[None, offset:ending]), axis=1)
    rank_sums = lax.all_to_all(
        sums.astype(jnp.bfloat16), "member", split_axis=0, concat_axis=2, tiled=True
    ).astype(jnp.float32)
    grad_count = (member_count - 1) * target_sign - rank_sums
    out_grad = (grad_count * cell_area[None, None, :] / float(member_count)).astype(jnp.bfloat16)
    pre_act = (
        jnp.einsum("io,min->mon", w_in_all, inputs, preferred_element_type=jnp.float32)
        + bias_in[None, :, None]
    )
    activated, slope = gelu_parts(pre_act)
    act_bf = activated.astype(jnp.bfloat16)
    act_grad = jnp.einsum("oc,mcn->mon", w_out_all, out_grad, preferred_element_type=jnp.float32)
    pre_grad = (act_grad * slope).astype(jnp.bfloat16)
    input_grad = jnp.einsum(
        "io,mon->min", w_in_all, pre_grad, preferred_element_type=jnp.float32
    ).astype(jnp.bfloat16)
    term_in = jnp.einsum("min,mon->io", inputs, pre_grad, preferred_element_type=jnp.float32)
    term_out = jnp.einsum("mon,mcn->oc", act_bf, out_grad, preferred_element_type=jnp.float32)
    term_bias = jnp.sum(pre_grad.astype(jnp.float32), axis=(0, 2))
    shares = (
        lax.psum_scatter(
            term_in.astype(jnp.bfloat16), "space", scatter_dimension=0, tiled=True
        ).astype(jnp.float32),
        lax.psum_scatter(
            term_out.astype(jnp.bfloat16), "space", scatter_dimension=0, tiled=True
        ).astype(jnp.float32),
        lax.psum_scatter(
            term_bias.astype(jnp.bfloat16), "space", scatter_dimension=0, tiled=True
        ).astype(jnp.float32),
    )
    reduced = (
        lax.psum(shares[0].astype(jnp.bfloat16), "member").astype(jnp.float32),
        lax.psum(shares[1].astype(jnp.bfloat16), "member").astype(jnp.float32),
        lax.psum(shares[2].astype(jnp.bfloat16), "member").astype(jnp.float32),
    )
    grad_scale = 1.0 / math.sqrt(member_count * cell_count)
    return (input_grad, reduced[0] * grad_scale, reduced[1] * grad_scale, reduced[2] * grad_scale)


def solution(mesh):
    return jax.shard_map(
        body,
        mesh=mesh,
        in_specs=(
            P("member", None, "space"),
            P("space", None),
            P(),
            P("space", None),
            P("member", None, "space"),
            P(None, "space"),
            P("space"),
        ),
        out_specs=(P("member", None, "space"), P("space", None), P("space", None), P("space")),
        check_vma=False,
    )
```

profile of v0, /device:TPU:33, one launch (start us, length us, event | category | flops | bytes accessed | tf_op | source)
XLA Modules:
  0.0 632.1 jit_solution(11367250266406768588)
XLA Ops:
  7.2 3.7 copy.53
  10.8 31.4 %all_to_all.24 = f32[4,87,1024]{1,0,2:T(4,128)S(1)} all-to-all(f32[4,87,1024]{1,0,2:T(4,128)} %copy.53), channel_id=1, replica_groups=mesh['member'=8,'space'=32] {'member'}, dimensions={2} | all-to-all | bytes 2850816 | tf_op jit(solution)/shard_map/all_to_all | solution.py:33
  42.3 0.9 copy.54
  43.2 0.1 fusion.26
  43.3 0.1 copy.55
  43.4 0.1 copy.56
  43.4 0.1 copy.57
  43.5 0.1 copy.58
  43.6 0.0 copy-start.4
  43.6 0.0 copy-start.6
  43.6 24.6 %sign_reduce_fusion.2 = (f32[32,87,128]{2,1,0:T(8,128)S(1)}, f32[32,87,128]{2,1,0:T(8,128)S(1)}, f32[32,87,128]{2,1,0:T(8,128)S(1)}, f32[32,87,128]{2,1,0:T(8,128)S(1)}) fusion(f32[8,87,128]{2,0,1:T(8,128)S(1)} %copy.56, f32[32,87,128]{2,1,0:T(8,128)S(1)} %bitcast.66, f32[8,87,128]{2,0,1:T(8,128)S(1)} %copy.57, f32[8,87,128]{2,0,1:T(8,128)S(1)} %copy.58, ...), kind=kLoop, calls=%fused_computation.4 | loop fusion | flops 32784384 | bytes 8552448 | tf_op jit(solution)/shard_map/reduce_sum | solution.py:37
  68.2 1.1 add_convert_fusion
  69.4 4.5 all-to-all-start.1
  73.8 0.0 reduce-scatter.7.cloned.1.call-start
  73.8 0.0 copy-done.4
  73.9 40.5 %all_gather.7 = bf16[512,512]{1,0:T(8,128)(2,1)S(1)} all-gather(bf16[16,512]{1,0:T(8,128)(2,1)S(1)} %copy-done.4), channel_id=1, replica_groups=mesh['member'=8,'space'=32] {'space'}, dimensions={0}, use_global_device_ids=true | all-gather | bytes 540672 | tf_op jit(solution)/shard_map/all_gather | solution.py:24
  114.4 0.0 copy-done.6
  114.4 31.5 %all_gather.6 = bf16[512,87]{1,0:T(8,128)(2,1)S(1)} all-gather(bf16[16,87]{1,0:T(8,128)(2,1)S(1)} %copy-done.6), channel_id=1, replica_groups=mesh['member'=8,'space'=32] {'space'}, dimensions={0}, use_global_device_ids=true | all-gather | bytes 91872 | tf_op jit(solution)/shard_map/all_gather | solution.py:25
  145.9 7.9 %fusion.19 = f32[4,1024,512]{2,1,0:T(8,128)} fusion(bf16[4,512,1024]{2,1,0:T(8,128)(2,1)} %param.7, bf16[512,512]{1,0:T(8,128)(2,1)S(1)} %all_gather.7), kind=kOutput, calls=%fused_computation.32 | convolution fusion | flops 2147483648 | bytes 13107200 | tf_op jit(solution)/shard_map/io,min->mon/dot_general | solution.py:44
  153.8 0.0 all-to-all-done.1
  153.8 0.1 convert_bitcast_fusion.1
  153.9 1.9 copy.59
  155.9 1.5 reshape.29
  157.3 0.0 copy-done
  157.4 2.1 fusion.13
  159.4 0.0 copy-start.1
  159.5 8.8 %fusion.27 = (bf16[512]{0:T(512)(128)(2,1)S(1)}, bf16[4,512,1024]{1,2,0:T(8,128)(2,1)S(1)}) fusion(f32[4,1024,512]{2,1,0:T(8,128)} %fusion.19, f32[512]{0:T(512)S(1)} %copy-done.7, bf16[4,87,1024]{2,1,0:T(8,128)(2,1)S(1)} %fusion.13, bf16[512,87]{1,0:T(8,128)(2,1)S(1)} %all_gather.6), kind=kOutput, calls=%fused_computation.43 | convolution fusion | flops 408944128 | bytes 13387776 | tf_op jit(solution)/shard_map/oc,mcn->mon/dot_general | solution.py:49
  168.3 0.0 copy-done.2
  168.3 0.0 copy-start.9
  168.3 2.0 copy-done.9
  170.3 2.4 fusion.15
  172.7 1.0 copy.68
  173.8 0.0 reduce-scatter.7.cloned.1.call-update
  173.8 0.3 reduce-scatter.5.cloned.1.call-start
  174.1 0.6 dynamic-slice
  175.3 6.2 fusion.17
  181.5 0.0 reduce-scatter.5.cloned.1.call-update
  181.6 6.5 %convert_bitcast_fusion = bf16[4,512,1024]{1,2,0:T(8,128)(2,1)} fusion(bf16[4,512,1024]{1,2,0:T(8,128)(2,1)} %copy-done.9, bf16[512,512]{1,0:T(8,128)(2,1)S(1)} %all_gather.7), kind=kOutput, calls=%fused_computation.15 | convolution fusion | flops 2149580800 | bytes 8912896 | tf_op jit(solution)/shard_map/io,mon->min/dot_general | solution.py:51
  188.0 6.2 copy.63
  194.2 54.3 %all-reduce = bf16[512]{0:T(512)(128)(2,1)S(1)} all-reduce(bf16[512]{0:T(512)(128)(2,1)S(1)} %get-tuple-element.39), channel_id=4, replica_groups=mesh['member'=8,'space'=32] {'space'}, use_global_device_ids=true, to_apply=%region_9.0.clone | all-reduce | flops 512 | bytes 2048
  248.5 0.1 dynamic-slice.1
  248.6 151.9 %reduce-scatter.7.cloned.1.call-done = bf16[16,512]{1,0:T(8,128)(2,1)} async-done(((bf16[512,512]{1,0:T(8,128)(2,1)}), bf16[16,512]{1,0:T(8,128)(2,1)}) %reduce-scatter.7.cloned.1.call-update) | async-done | bytes 16400
  400.5 0.8 copy.69
  401.4 193.9 %reduce-scatter.5.cloned.1.call-done = bf16[16,87]{1,0:T(8,128)(2,1)} async-done(((bf16[512,87]{1,0:T(8,128)(2,1)}), bf16[16,87]{1,0:T(8,128)(2,1)}) %reduce-scatter.5.cloned.1.call-update) | async-done | bytes 2800 | tf_op jit(solution)/shard_map/reduce_scatter | solution.py:61
  595.3 28.1 %all-reduce.1 = (bf16[16,512]{0,1:T(8,128)(2,1)S(1)}, bf16[16,87]{1,0:T(8,128)(2,1)S(1)}, bf16[16]{0:T(256)(128)(2,1)S(1)}) all-reduce(bf16[16,512]{0,1:T(8,128)(2,1)S(1)} %copy.69, bf16[16,87]{1,0:T(8,128)(2,1)} %reduce-scatter.5.cloned.1.call-done, bf16[16]{0:T(256)(128)(2,1)S(1)} %dynamic-slice.1), channel_id=1, replica_groups=mesh['member'=8,'space'=32] {'member'}, use_global_device_ids=true, to_apply=%region_5.0 | all-reduce | flops 9600 | bytes 38400 | tf_op jit(solution)/shard_map/psum | solution.py:69
  623.5 0.7 copy.64
  624.2 0.6 convert_multiply_fusion.1
  624.8 0.5 convert_multiply_fusion.2
  (12 shorter events, 0.0 us)
Async XLA Ops:
  43.6 30.2 %copy-start.4 = (bf16[16,512]{1,0:T(8,128)(2,1)S(1)}, bf16[16,512]{1,0:T(8,128)(2,1)}, u32[]{:S(2)}) copy-start(bf16[16,512]{1,0:T(8,128)(2,1)} %param.8) | copy-start | bytes 49156
  43.6 70.7 %copy-start.6 = (bf16[16,87]{1,0:T(8,128)(2,1)S(1)}, bf16[16,87]{1,0:T(8,128)(2,1)}, u32[]{:S(2)}) copy-start(bf16[16,87]{1,0:T(8,128)(2,1)} %param.10) | copy-start | bytes 8356
  69.4 84.5 %all-to-all-start.1 = ((bf16[32,87,128]{2,1,0:T(8,128)(2,1)}), bf16[32,87,128]{2,1,0:T(8,128)(2,1)S(1)}, u32[]{:S(2)}, u32[]{:S(2)}) async-start(bf16[32,87,128]{2,1,0:T(8,128)(2,1)} %add_convert_fusion), calls=%async_computation.1 | async-start | bytes 1441792 | tf_op jit(solution)/shard_map/all_to_all | solution.py:38
  73.8 326.7 %reduce-scatter.7.cloned.1.call-start = ((), (), s32[]{:S(2)}) async-start(), calls=%async_computation.5 | async-start | bytes 540672
  145.9 11.5 %copy-start = (f32[4,87,1024]{2,0,1:T(4,128)S(1)}, f32[4,87,1024]{2,0,1:T(4,128)}, u32[]{:S(2)}) copy-start(f32[4,87,1024]{2,0,1:T(4,128)} %param.11) | copy-start | bytes 4276228
  145.9 11.5 %copy-start.5 = (f32[1024]{0:T(1024)S(1)}, f32[1024]{0:T(1024)}, u32[]{:S(2)}) copy-start(f32[1024]{0:T(1024)} %param.13) | copy-start | bytes 12292
  153.8 5.6 copy-start.7
  159.4 8.9 %copy-start.2 = (bf16[4,87,1024]{2,1,0:T(8,128)(2,1)}, bf16[4,87,1024]{2,1,0:T(8,128)(2,1)S(1)}, u32[]{:S(2)}) copy-start(bf16[4,87,1024]{2,1,0:T(8,128)(2,1)S(1)} %fusion.13) | copy-start | bytes 2138116
  159.4 10.9 %copy-start.1 = (bf16[4,512,1024]{2,1,0:T(8,128)(2,1)S(1)}, bf16[4,512,1024]{2,1,0:T(8,128)(2,1)}, u32[]{:S(2)}) copy-start(bf16[4,512,1024]{2,1,0:T(8,128)(2,1)} %param.7) | copy-start | bytes 12582916
  168.3 2.0 copy-start.9
  170.3 3.7 copy-start.8
  170.3 5.0 copy-start.3
  173.8 421.5 %reduce-scatter.5.cloned.1.call-start = ((), (), s32[]{:S(2)}) async-start(), calls=%async_computation.4 | async-start | bytes 135168 | tf_op jit(solution)/shard_map/reduce_scatter | solution.py:61
Sparse Core Ops, SparseCore 0:
  173.9 226.5 reduce-scatter.6
  404.6 190.6 reduce-scatter.4
where the time goes:
time: 636 us; the launch traced here: 632 us
  waiting for transfers between devices  346 us (54%)
  blocking collectives  186 us (29%)
  matrix products  31.8 us (5%)
  other arithmetic  29 us (5%)
  local copies, waits for them, and re-layouts  19.9 us (3%)
  between operations  14.9 us (2%)
    reduce_scatter x1, waiting for transfers between devices, body(): lax.psum_scatter(term_out.astype(jnp.bfloat16), 'space', scatter_dimensio...  194 us
    unnamed x3, waiting for transfers between devices  152 us
    unnamed x1, blocking collectives  54.3 us
    all_gather x1, blocking collectives, body(): lax.all_gather(w_in, 'space', axis=0, tiled=True)  40.5 us
    all_gather x1, blocking collectives, body(): lax.all_gather(w_out, 'space', axis=0, tiled=True)  31.5 us
    all_to_all x1, blocking collectives, body(): lax.all_to_all(members_out, 'member', split_axis=2, concat_axis=0, tiled=...  31.4 us
    psum x1, blocking collectives, body(): lax.psum(shares[0].astype(jnp.bfloat16), 'member').astype(jnp.float32)  28.1 us
    reduce_sum x1, other arithmetic, body(): jnp.sum(jnp.sign(gathered[:, None] - gathered[None, offset:ending]), axis=1)  24.6 us
  transfers between devices with their start and end apart: 3, of which 2 were waited for; matrix products, arithmetic and copies ran while one was open for 4% of the time, Pallas kernels for 0%

commit v1 on v0

v1 whole, which is shorter than its diff:
```python
import functools
import math

import jax
import jax.numpy as jnp
from jax import lax
from jax.experimental import pallas as pl
from jax.experimental.pallas import tpu as pltpu
from jax.sharding import PartitionSpec as P

CUBIC = 0.044715
ROOT = 0.7978845608028654
MESH = pl.DeviceIdType.MESH
F32 = jnp.float32
BF16 = jnp.bfloat16
LANES = 128


def dot_nn(a, b):
    return jnp.dot(a, b, preferred_element_type=F32)


def dot_nt(a, b):
    return lax.dot_general(a, b, (((1,), (1,)), ((), ())), preferred_element_type=F32)


def kernel(
    members_n, spaces_n, chan, scale,
    x_hbm, w_hbm, bias_ref, wo_hbm, mem_hbm, tgt_hbm, area_ref,
    ig_hbm, win_out, wout_out, bias_out,
    x, w, wt, wo, wop, bias_b, got, last, tgt, back, og, act, slope, pg, ig,
    acc_in, acc_out, acc_b, part, pair, total, spread, owned, shares,
    load_sem, w_sem, w_send, a2a_recv, a2a_send, a2a_own, back_recv, back_send, back_own,
    pair_sem, red_recv, red_send, red_own, fin_recv, fin_send, fin_own, out_sem,
):
    me = lax.axis_index("member")
    here = lax.axis_index("space")
    core = lax.rem(me, 2)
    own_m, hid, cells = x.shape
    rows = w_hbm.shape[0]
    half_spaces = spaces_n // 2
    chips = members_n // 2
    count = own_m * members_n
    wide = acc_in.shape[1]

    def member_peer(k):
        return lax.rem(me + k, members_n)

    def space_peer(k):
        return lax.rem(here + k, spaces_n)

    barrier = pltpu.get_barrier_semaphore()

    def greet_space(k, _):
        pl.semaphore_signal(barrier, inc=1, device_id={"space": space_peer(k)}, device_id_type=MESH)
        return 0

    def greet_member(k, _):
        pl.semaphore_signal(barrier, inc=1, device_id={"member": member_peer(k)}, device_id_type=MESH)
        return 0

    loads = [pltpu.make_async_copy(x_hbm.at[m], x.at[m], load_sem.at[m]) for m in range(own_m)]
    own_cells = pl.ds(pl.multiple_of(me * LANES, LANES), LANES)
    tgt_load = pltpu.make_async_copy(tgt_hbm.at[:, own_cells], tgt, load_sem.at[own_m])
    lax.fori_loop(1, members_n, greet_member, 0)
    lax.fori_loop(1, spaces_n, greet_space, 0)
    tgt_load.start()
    pl.semaphore_wait(barrier, members_n + spaces_n - 2)

    cuts = ((0, 48), (48, chan))
    own_slots = pl.ds(pl.multiple_of(me * own_m, own_m), own_m)

    def values_to(k, part_at):
        lo, hi = cuts[part_at]
        peer = member_peer(k)
        return pltpu.make_async_remote_copy(
            src_ref=mem_hbm.at[:, lo:hi, pl.ds(pl.multiple_of(peer * LANES, LANES), LANES)],
            dst_ref=got.at[own_slots, lo:hi, :],
            send_sem=a2a_send.at[part_at],
            recv_sem=a2a_recv.at[part_at],
            device_id={"member": peer},
            device_id_type=MESH,
        )

    def own_values(part_at):
        lo, hi = cuts[part_at]
        return pltpu.make_async_copy(
            mem_hbm.at[:, lo:hi, own_cells], got.at[own_slots, lo:hi, :], a2a_own.at[part_at]
        )

    for part_at in range(2):
        for k in range(1, members_n):
            values_to(k, part_at).start()
        own_values(part_at).start()

    own_rows = pl.ds(pl.multiple_of(here * rows, rows), rows)

    def send_rows(k, _):
        peer = space_peer(k)
        pltpu.make_async_remote_copy(
            src_ref=w_hbm, dst_ref=w.at[own_rows, :], send_sem=w_send.at[0], recv_sem=w_sem.at[0],
            device_id={"space": peer}, device_id_type=MESH,
        ).start()
        pltpu.make_async_remote_copy(
            src_ref=wo_hbm, dst_ref=wo.at[own_rows, :], send_sem=w_send.at[1], recv_sem=w_sem.at[1],
            device_id={"space": peer}, device_id_type=MESH,
        ).start()
        return 0

    lax.fori_loop(1, spaces_n, send_rows, 0)
    own_w = pltpu.make_async_copy(w_hbm, w.at[own_rows, :], w_sem.at[2])
    own_wo = pltpu.make_async_copy(wo_hbm, wo.at[own_rows, :], w_sem.at[3])
    own_w.start()
    own_wo.start()
    for load in loads:
        load.start()

    bias_b[...] = jnp.broadcast_to(bias_ref[...], (LANES, hid)).T
    og[:, 96:, :] = jnp.zeros((own_m, og.shape[1] - 96, cells), BF16)
    wop[...] = jnp.zeros(wop.shape, BF16)
    last[...] = jnp.zeros(last.shape, F32)
    acc_in[...] = jnp.zeros(acc_in.shape, F32)
    acc_out[...] = jnp.zeros(acc_out.shape, F32)
    acc_b[...] = jnp.zeros(acc_b.shape, F32)

    tgt_load.wait()
    own_w.wait()
    own_wo.wait()
    others = (spaces_n - 1) * rows
    pltpu.make_async_copy(w.at[0:others, :], w.at[0:others, :], w_sem.at[0]).wait()
    pltpu.make_async_copy(wo.at[0:others, :], wo.at[0:others, :], w_sem.at[1]).wait()
    wt[...] = w[...].T
    wop[:, 0:chan] = wo[...]

    nb = 256
    blocks = cells // nb

    def forward(m):
        loads[m].wait()

        def step(b, _):
            at = pl.ds(pl.multiple_of(b * nb, nb), nb)
            bias2 = jnp.concatenate([bias_b[...]] * (nb // LANES), axis=1)
            v = dot_nn(wt[...], x[m, :, at]) + bias2
            sq = v * v
            u = 0.5 + 0.5 * jnp.tanh(v * (ROOT + (ROOT * CUBIC) * sq))
            a = v * u
            act[m, :, at] = a.astype(BF16)
            slope[m, :, at] = (u + a * (1.0 - u) * (2.0 * ROOT + (6.0 * ROOT * CUBIC) * sq)).astype(BF16)
            return 0

        lax.fori_loop(0, blocks, step, 0)

    area_row = area_ref[:, own_cells] * (1.0 / count)

    def rank_tile(load, target, store):
        values = [load(k) for k in range(count)]
        less = [None] * count
        for a in range(count):
            for b in range(a + 1, count):
                above = jnp.where(values[a] > values[b], 1.0, 0.0)
                less[a] = above if less[a] is None else less[a] + above
                less[b] = (float(b) - above) if less[b] is None else less[b] - above
        for a in range(count):
            grad = jnp.where(values[a] > target, float(2 * (count - 1)), 0.0) - 2.0 * less[a]
            store(a, grad * area_row)

    grads = spread

    def rank_rows(tile, _):
        at = pl.ds(pl.multiple_of(tile * 8, 8), 8)

        def store(k, value):
            grads[k, at, :] = value

        rank_tile(lambda k: got[k, at, :], tgt[at, :], store)
        return 0

    def pack(first, ending):
        def step(k, _):
            back[k, first:ending, :] = grads[k, first:ending, :].astype(BF16)
            return 0

        lax.fori_loop(0, count, step, 0)

    packs = ((0, 48), (48, 96))

    def grads_to(k, part_at):
        lo, hi = packs[part_at]
        peer = member_peer(k)
        return pltpu.make_async_remote_copy(
            src_ref=back.at[pl.ds(pl.multiple_of(peer * own_m, own_m), own_m), lo:hi, :],
            dst_ref=og.at[:, lo:hi, own_cells],
            send_sem=back_send.at[part_at],
            recv_sem=back_recv.at[part_at],
            device_id={"member": peer},
            device_id_type=MESH,
        )

    def own_grads(part_at):
        lo, hi = packs[part_at]
        return pltpu.make_async_copy(
            back.at[own_slots, lo:hi, :], og.at[:, lo:hi, own_cells], back_own.at[part_at]
        )

    def wait_values(part_at):
        lo, hi = cuts[part_at]
        own_values(part_at).wait()
        rest = got.at[0 : count - own_m, lo:hi, :]
        pltpu.make_async_copy(rest, rest, a2a_recv.at[part_at]).wait()

    def send_grads(part_at):
        for k in range(1, members_n):
            grads_to(k, part_at).start()
        own_grads(part_at).start()

    for m in range(own_m // 2):
        forward(m)
    wait_values(0)
    lax.fori_loop(0, 6, rank_rows, 0)
    pack(0, 48)
    send_grads(0)
    for m in range(own_m // 2, own_m):
        forward(m)
    wait_values(1)
    full = chan // 8
    lax.fori_loop(6, full, rank_rows, 0)
    tail = chan - full * 8
    for k in range(count):
        last[k, 0:tail, :] = got[k, full * 8 : chan, :]
    last[count, 0:tail, :] = tgt[full * 8 : chan, :]
    keep = lax.broadcasted_iota(jnp.int32, (8, LANES), 0) < tail

    def store_last(k, value):
        grads[k, full * 8 : full * 8 + 8, :] = jnp.where(keep, value, 0.0)
        grads[k, full * 8 + 8 : 96, :] = jnp.zeros((96 - full * 8 - 8, LANES), F32)

    rank_tile(lambda k: last[k], last[count], store_last)
    pack(48, 96)
    send_grads(1)

    for part_at in range(2):
        lo, hi = packs[part_at]
        own_grads(part_at).wait()
        rest = og.at[:, lo:hi, 0 : cells - LANES]
        pltpu.make_async_copy(rest, rest, back_recv.at[part_at]).wait()

    nc = 512

    def weight_terms(m, _):
        for b in range(cells // nc):
            at = slice(b * nc, (b + 1) * nc)
            p = dot_nn(wop[...], og[m, :, at]) * slope[m, :, at].astype(F32)
            pg[m, :, at] = p.astype(BF16)
            folded = p[:, 0:LANES]
            for c in range(1, nc // LANES):
                folded = folded + p[:, c * LANES : (c + 1) * LANES]
            acc_b[...] += folded
        acc_in[...] += dot_nt(x[m], pg[m])
        acc_out[...] += dot_nt(act[m], og[m])
        return 0

    lax.fori_loop(0, own_m, weight_terms, 0)

    lane = lax.broadcasted_iota(jnp.int32, (hid, LANES), 1)
    summed = jnp.sum(acc_b[...], axis=1, keepdims=True)
    acc_out[...] = jnp.where(lane == chan, summed, acc_out[...])

    half = hid // 2
    mine = pl.ds(pl.multiple_of(core * half, half), half)
    theirs = pl.ds(pl.multiple_of((1 - core) * half, half), half)
    part[:, 0:wide] = acc_in[theirs, :].astype(BF16)
    part[:, wide:] = acc_out[theirs, :].astype(BF16)
    sibling = me + 1 - 2 * core
    to_sibling = pltpu.make_async_remote_copy(
        src_ref=part, dst_ref=pair, send_sem=pair_sem.at[0], recv_sem=pair_sem.at[1],
        device_id={"member": sibling}, device_id_type=MESH,
    )
    to_sibling.start()

    def input_grads(m):
        def step(b, _):
            at = pl.ds(pl.multiple_of(b * nb, nb), nb)
            ig[m, :, at] = dot_nn(w[...], pg[m, :, at]).astype(BF16)
            return 0

        lax.fori_loop(0, blocks, step, 0)
        pltpu.make_async_copy(ig.at[m], ig_hbm.at[m], out_sem.at[m]).start()

    to_sibling.wait_recv()
    total[:, 0:wide] = (acc_in[mine, :] + pair[:, 0:wide].astype(F32)).astype(BF16)
    total[:, wide:] = (acc_out[mine, :] + pair[:, wide:].astype(F32)).astype(BF16)

    owner_core = here // half_spaces
    own_at = lax.rem(here, half_spaces)
    owner = owner_core == core

    def block_to(t):
        return pltpu.make_async_remote_copy(
            src_ref=total.at[pl.ds(pl.multiple_of(t * rows, rows), rows), :],
            dst_ref=shares.at[here],
            send_sem=red_send, recv_sem=red_recv,
            device_id={"space": core * half_spaces + t}, device_id_type=MESH,
        )

    own_block = pltpu.make_async_copy(
        total.at[pl.ds(pl.multiple_of(own_at * rows, rows), rows), :], shares.at[here], red_own
    )

    @pl.when(owner)
    def _():
        def send(k, _):
            block_to(lax.rem(own_at + k, half_spaces)).start()
            return 0

        lax.fori_loop(1, half_spaces, send, 0)
        own_block.start()

    @pl.when(jnp.logical_not(owner))
    def _():
        def send(k, _):
            block_to(lax.rem(own_at + k, half_spaces)).start()
            return 0

        lax.fori_loop(0, half_spaces, send, 0)

    for m in range(own_m - 1):
        input_grads(m)

    chip = me // 2

    def sum_to(k):
        return pltpu.make_async_remote_copy(
            src_ref=owned.at[chips], dst_ref=owned.at[chip], send_sem=fin_send, recv_sem=fin_recv,
            device_id={"member": member_peer(k)}, device_id_type=MESH,
        )

    own_sum = pltpu.make_async_copy(owned.at[chips], owned.at[chip], fin_own)

    @pl.when(owner)
    def _():
        own_block.wait()
        rest = shares.at[0 : spaces_n - 1]
        pltpu.make_async_copy(rest, rest, red_recv).wait()
        value = shares[0].astype(F32)
        for k in range(1, spaces_n):
            value = value + shares[k].astype(F32)
        owned[chips] = value.astype(BF16)
        for k in range(1, members_n):
            sum_to(k).start()
        own_sum.start()

    input_grads(own_m - 1)

    @pl.when(owner)
    def _():
        own_sum.wait()
        rest = owned.at[0 : chips - 1]
        pltpu.make_async_copy(rest, rest, fin_recv).wait()

    @pl.when(jnp.logical_not(owner))
    def _():
        rest = owned.at[0:chips]
        pltpu.make_async_copy(rest, rest, fin_recv).wait()

    result = owned[0].astype(F32)
    for k in range(1, chips):
        result = result + owned[k].astype(F32)
    result = result * scale
    win_out[...] = result[:, 0:wide]
    wout_out[...] = result[:, wide : wide + chan]
    column = result[:, wide + chan : wide + chan + 1]
    eye = lax.broadcasted_iota(jnp.int32, (rows, rows), 0) == lax.broadcasted_iota(jnp.int32, (rows, rows), 1)
    bias_out[...] = jnp.sum(jnp.where(eye, column, 0.0), axis=0, keepdims=True)

    for part_at in range(2):
        lo, hi = cuts[part_at]
        rest = got.at[0 : count - own_m, lo:hi, :]
        pltpu.make_async_copy(rest, rest, a2a_send.at[part_at]).wait()
        lo, hi = packs[part_at]
        rest = back.at[0 : count - own_m, lo:hi, :]
        pltpu.make_async_copy(rest, rest, back_send.at[part_at]).wait()
    pltpu.make_async_copy(w.at[0:others, :], w.at[0:others, :], w_send.at[0]).wait()
    pltpu.make_async_copy(wo.at[0:others, :], wo.at[0:others, :], w_send.at[1]).wait()
    to_sibling.wait_send()

    @pl.when(owner)
    def _():
        rest = total.at[0 : (half_spaces - 1) * rows, :]
        pltpu.make_async_copy(rest, rest, red_send).wait()
        rest = shares.at[0 : members_n - 1]
        pltpu.make_async_copy(rest, rest, fin_send).wait()

    @pl.when(jnp.logical_not(owner))
    def _():
        pltpu.make_async_copy(total, total, red_send).wait()

    for m in range(own_m):
        pltpu.make_async_copy(ig.at[m], ig_hbm.at[m], out_sem.at[m]).wait()


def body(members_n, spaces_n, inputs, w_in, bias_in, w_out, members_out, target, cell_area):
    own_m, hid, cells = inputs.shape
    rows, chan = w_out.shape
    count = own_m * members_n
    padded = LANES
    wide = w_in.shape[1]
    scale = 1.0 / math.sqrt(count * cells * spaces_n)
    chips = members_n // 2
    any_spec = pl.BlockSpec(memory_space=pl.ANY)
    vmem_spec = pl.BlockSpec(memory_space=pltpu.VMEM)
    dma = pltpu.SemaphoreType.DMA
    hidden = (own_m, hid, cells)
    outs = pl.pallas_call(
        functools.partial(kernel, members_n, spaces_n, chan, scale),
        out_shape=(
            jax.ShapeDtypeStruct(hidden, BF16),
            jax.ShapeDtypeStruct((rows, wide), F32),
            jax.ShapeDtypeStruct((rows, chan), F32),
            jax.ShapeDtypeStruct((1, rows), F32),
        ),
        in_specs=[any_spec, any_spec, vmem_spec, any_spec, any_spec, any_spec, vmem_spec],
        out_specs=(any_spec, vmem_spec, vmem_spec, vmem_spec),
        scratch_shapes=[
            pltpu.VMEM(hidden, BF16),
            pltpu.VMEM((hid, wide), BF16),
            pltpu.VMEM((wide, hid), BF16),
            pltpu.VMEM((hid, chan), BF16),
            pltpu.VMEM((hid, padded), BF16),
            pltpu.VMEM((hid, LANES), F32),
            pltpu.VMEM((count, chan, LANES), F32),
            pltpu.VMEM((count + 1, 8, LANES), F32),
            pltpu.VMEM((chan, LANES), F32),
            pltpu.VMEM((count, 96, LANES), BF16),
            pltpu.VMEM((own_m, padded, cells), BF16),
            pltpu.VMEM(hidden, BF16),
            pltpu.VMEM(hidden, BF16),
            pltpu.VMEM(hidden, BF16),
            pltpu.VMEM(hidden, BF16),
            pltpu.VMEM((hid, wide), F32),
            pltpu.VMEM((hid, LANES), F32),
            pltpu.VMEM((hid, LANES), F32),
            pltpu.VMEM((hid // 2, wide + LANES), BF16),
            pltpu.VMEM((hid // 2, wide + LANES), BF16),
            pltpu.VMEM((hid // 2, wide + LANES), BF16),
            pltpu.VMEM((count, 96, LANES), F32),
            pltpu.VMEM((chips + 1, rows, wide + LANES), BF16),
            pltpu.VMEM((spaces_n, rows, wide + LANES), BF16),
            dma((own_m + 1,)),
            dma((4,)),
            dma((2,)),
            dma((2,)),
            dma((2,)),
            dma((2,)),
            dma((2,)),
            dma((2,)),
            dma((2,)),
            dma((2,)),
            dma,
            dma,
            dma,
            dma,
            dma,
            dma,
            dma((own_m,)),
        ],
        compiler_params=pltpu.CompilerParams(
            collective_id=0, has_side_effects=True, vmem_limit_bytes=60 * 1024 * 1024
        ),
        name="crps_backward",
    )(
        inputs, w_in, bias_in.reshape(1, -1), w_out, members_out, target, cell_area.reshape(1, -1)
    )
    return outs[0], outs[1], outs[2], outs[3].reshape(rows)


def solution(mesh):
    members_n, spaces_n = mesh.shape["member"], mesh.shape["space"]
    return jax.shard_map(
        functools.partial(body, members_n, spaces_n),
        mesh=mesh,
        in_specs=(
            P("member", None, "space"),
            P("space", None),
            P(),
            P("space", None),
            P("member", None, "space"),
            P(None, "space"),
            P("space"),
        ),
        out_specs=(P("member", None, "space"), P("space", None), P("space", None), P("space")),
        check_vma=False,
    )
```

time: 636 us -> 78.6 us (0.12)
  waiting for transfers between devices: 346 us -> 0 us
  blocking collectives: 186 us -> 0 us
  Pallas kernels: 0 us -> 67.6 us
  matrix products: 31.8 us -> 0 us
  other arithmetic: 29 us -> 0 us
  between operations: 14.9 us -> 0.67 us
  local copies, waits for them, and re-layouts: 19.9 us -> 9.67 us
    reduce_scatter x1 -> x0, waiting for transfers between devices: 194 us -> none  [body(): lax.psum_scatter(term_out.astype(jnp.bfloat16), 'space', scatter_dimensio...]
    unnamed x3 -> x0, waiting for transfers between devices: 152 us -> none
    all_gather x2 -> x0, blocking collectives: 72 us -> none  [the longest x1 40.5 us: body(): lax.all_gather(w_in, 'space', axis=0, tiled=True)]
    pallas_call x0 -> x1, Pallas kernels: none -> 67.6 us  [body(): pl.pallas_call(functools.partial(kernel, members_n, spaces_n, chan, scale...]
    unnamed x1 -> x0, blocking collectives: 54.3 us -> none
    dot_general x5 -> x0, matrix products: 31.8 us -> none  [the longest x1 8.84 us: body(): jnp.einsum('oc,mcn->mon', w_out_all, out_grad, preferred_element_type=jnp...]
    all_to_all x1 -> x0, blocking collectives: 31.4 us -> none  [body(): lax.all_to_all(members_out, 'member', split_axis=2, concat_axis=0, tiled=...]
    psum x1 -> x0, blocking collectives: 28.1 us -> none  [body(): lax.psum(shares[0].astype(jnp.bfloat16), 'member').astype(jnp.float32)]
  transfers between devices with their start and end apart: 3 -> 0, of which waited for: 2 -> 0; matrix products, arithmetic and copies ran while one was open for 4% -> 0% of each run, Pallas kernels for 0% -> 0%
where the time goes in v1:
time: 78.6 us; the launch traced here: 78 us
  Pallas kernels  67.6 us (86%)
  local copies, waits for them, and re-layouts  9.67 us (12%)
    pallas_call x1, Pallas kernels, body(): pl.pallas_call(functools.partial(kernel, members_n, spaces_n, chan, scale...  67.6 us
    unnamed x11, local copies, waits for them, and re-layouts  9.67 us

profile of v1, /device:TPU:33, one launch (start us, length us, event | category | flops | bytes accessed | tf_op | source)
XLA Modules:
  0.0 78.0 jit_solution(6888697058591311115)
XLA Ops:
  0.6 3.3 %copy.11.mem_hbm = f32[4,87,1024]{2,1,0:T(8,128)} copy(f32[4,87,1024]{2,0,1:T(4,128)} %param.11) | data formatting | bytes 2850816 | tf_op args[4]
  3.9 67.6 %crps_backward.1 = (bf16[4,512,1024]{2,1,0:T(8,128)(2,1)}, f32[16,512]{1,0:T(8,128)}, f32[16,87]{1,0:T(8,128)}, f32[1,16]{1,0:T(1,128)}) custom-call(bf16[4,512,1024]{2,1,0:T(8,128)(2,1)} %x_hbm.1, bf16[16,512]{1,0:T(8,128)(2,1)} %w_hbm.1, f32[1,512]{1,0:T(1,128)} %bitcast.4, bf16[16,87]{1,0:T(8,128)(2,1)} %wo_hbm.1, f32[4,87,1024]{2,1,0:T(8,128)} %copy.11.mem_hbm, ...), custom_call_target="tpu_custom_call" | custom-call | tf_op jit(solution)/shard_map/crps_backward/pallas_call | solution.py:414
  71.6 0.0 copy-start
  71.6 0.0 copy-start.1
  71.6 0.0 copy-start.2
  71.6 4.6 %copy.16 = bf16[4,512,1024]{2,1,0:T(8,128)(2,1)} copy(bf16[4,512,1024]{2,1,0:T(8,128)(2,1)} %get-tuple-element.16) | data formatting | bytes 8388608
  76.2 0.0 copy-done
  76.2 0.6 copy.17
  76.9 0.0 copy-done.1
  76.9 0.6 copy.18
  77.5 0.0 copy-done.2
  77.5 0.5 copy.19
Async XLA Ops:
  71.6 4.7 %copy-start = (f32[16,512]{1,0:T(8,128)S(1)}, f32[16,512]{1,0:T(8,128)}, u32[]{:S(2)}) copy-start(f32[16,512]{1,0:T(8,128)} %get-tuple-element.17) | copy-start | bytes 98308
  71.6 5.3 %copy-start.1 = (f32[16,87]{1,0:T(8,128)S(1)}, f32[16,87]{1,0:T(8,128)}, u32[]{:S(2)}) copy-start(f32[16,87]{1,0:T(8,128)} %get-tuple-element.18) | copy-start | bytes 16708
  71.6 5.9 %copy-start.2 = (f32[1,16]{1,0:T(1,128)S(1)}, f32[1,16]{1,0:T(1,128)}, u32[]{:S(2)}) copy-start(f32[1,16]{1,0:T(1,128)} %get-tuple-element.11) | copy-start | bytes 196

commit v2 on v0

v2 whole, which is shorter than its diff:
```python
import functools
import math

import jax
import jax.numpy as jnp
from jax import lax
from jax.experimental import pallas as pl
from jax.experimental.pallas import tpu as pltpu
from jax.sharding import PartitionSpec as P

CUBIC = 0.044715
ROOT = 0.7978845608028654
MESH = pl.DeviceIdType.MESH
F32 = jnp.float32
BF16 = jnp.bfloat16
LANES = 128
HALF_ROWS = 48


def dot_nn(a, b):
    return jnp.dot(a, b, preferred_element_type=F32)


def dot_nt(a, b):
    return lax.dot_general(a, b, (((1,), (1,)), ((), ())), preferred_element_type=F32)


def kernel(
    members_n, spaces_n, chan, scale,
    x_hbm, w_hbm, bias_hbm, wo_hbm, mem_hbm, tgt_hbm, area_hbm,
    ig, result_out,
    x, bias_ref, area_ref, stage, wo_raw, wo_wide, wall, wt, bias_b, got, flat, tgt_raw, tgt, grads, back, og, act, slope, pg,
    acc_in, acc_out, acc_b, part, pair, total, shares, owned,
    load_sem, w_recv, w_send, a2a_recv, a2a_send, a2a_own, back_recv, back_send, back_own,
    pair_sem, red_recv, red_send, fin_recv, fin_send,
):
    me = lax.axis_index("member")
    here = lax.axis_index("space")
    core = lax.rem(me, 2)
    own_m, hid, cells = x.shape
    rows = w_hbm.shape[0]
    half_spaces = spaces_n // 2
    half_members = members_n // 2
    half_hid = hid // 2
    half_cells = cells // 2
    count = own_m * members_n
    wide = wt.shape[0]
    half_chan = got.shape[2]
    my_half = lax.rem(here // half_spaces + core, 2)
    sibling = me + 1 - 2 * core

    def member_peer(k):
        return lax.rem(me + k, members_n)

    def space_peer(k):
        return my_half * half_spaces + lax.rem(here + k, half_spaces)

    barrier = pltpu.get_barrier_semaphore()

    def greet_space(k, _):
        pl.semaphore_signal(barrier, inc=1, device_id={"space": space_peer(k)}, device_id_type=MESH)
        return 0

    def greet_member(k, _):
        pl.semaphore_signal(barrier, inc=1, device_id={"member": member_peer(k)}, device_id_type=MESH)
        return 0

    first = 1 - core
    lax.fori_loop(first, half_spaces, greet_space, 0)
    lax.fori_loop(1, members_n, greet_member, 0)

    load_w = pltpu.make_async_copy(w_hbm, stage.at[:, 0:wide], load_sem.at[own_m])
    load_wo = pltpu.make_async_copy(wo_hbm, wo_raw, load_sem.at[own_m + 1])
    load_tgt = pltpu.make_async_copy(tgt_hbm, tgt_raw, load_sem.at[own_m + 2])
    load_bias = pltpu.make_async_copy(bias_hbm, bias_ref, load_sem.at[own_m + 3])
    load_area = pltpu.make_async_copy(area_hbm, area_ref, load_sem.at[own_m + 4])
    loads = [pltpu.make_async_copy(x_hbm.at[m], x.at[m], load_sem.at[m]) for m in range(own_m)]
    load_w.start()
    load_wo.start()
    load_tgt.start()
    load_bias.start()
    load_area.start()
    for load in loads:
        load.start()

    wo_wide[...] = jnp.zeros(wo_wide.shape, F32)
    load_wo.wait()
    wo_wide[:, 0:half_chan] = wo_raw[:, 0:half_chan].astype(F32)
    second = HALF_ROWS + 2 * half_chan - chan
    wo_wide[:, second : second + chan - half_chan] = wo_raw[:, half_chan:chan].astype(F32)
    stage[:, wide:] = wo_wide[...].astype(BF16)
    load_w.wait()

    pl.semaphore_wait(barrier, members_n - 1 + half_spaces - first)

    def place(peer, chunk):
        channel_half = lax.rem(peer // half_members + chunk, 2)
        tile = lax.rem(peer, half_members) + chunk * half_members
        return channel_half, pl.ds(pl.multiple_of(tile * LANES, LANES), LANES)

    def values_from(peer, chunk):
        channel_half, at = place(peer, chunk)
        return mem_hbm.at[pl.ds(channel_half * (chan - half_chan), half_chan), :, at]

    def values_to(k, chunk):
        peer = member_peer(k)
        return pltpu.make_async_remote_copy(
            src_ref=values_from(peer, chunk),
            dst_ref=got.at[chunk, me],
            send_sem=a2a_send.at[chunk],
            recv_sem=a2a_recv.at[chunk],
            device_id={"member": peer},
            device_id_type=MESH,
        )

    def own_values(chunk):
        return pltpu.make_async_copy(values_from(me, chunk), got.at[chunk, me], a2a_own.at[chunk])

    def send_values(chunk):
        for k in range(1, members_n):
            values_to(k, chunk).start()
        own_values(chunk).start()

    def send_rows(k, _):
        pltpu.make_async_remote_copy(
            src_ref=stage, dst_ref=wall.at[here], send_sem=w_send.at[0], recv_sem=w_recv.at[0],
            device_id={"space": space_peer(k)}, device_id_type=MESH,
        ).start()
        return 0

    send_values(0)
    lax.fori_loop(first, half_spaces, send_rows, 0)

    @pl.when(core == 0)
    def _():
        pltpu.make_async_copy(stage, wall.at[here], w_recv.at[0]).start()

    send_values(1)

    load_bias.wait()
    load_area.wait()
    bias_b[...] = jnp.broadcast_to(bias_ref[...], (LANES, hid)).T
    og[:, 2 * HALF_ROWS :, :] = jnp.zeros((own_m, og.shape[1] - 2 * HALF_ROWS, cells), BF16)
    flat[...] = jnp.zeros(flat.shape, F32)
    tgt[...] = jnp.zeros(tgt.shape, F32)
    acc_in[...] = jnp.zeros(acc_in.shape, F32)
    acc_out[...] = jnp.zeros(acc_out.shape, F32)
    acc_b[...] = jnp.zeros(acc_b.shape, F32)
    load_tgt.wait()
    tgt[0, 0:half_chan, :] = tgt_raw[0:half_chan, :]
    tgt[1, 0:half_chan, :] = tgt_raw[chan - half_chan : chan, :]

    mine_w = wall.at[pl.ds(my_half * half_spaces, half_spaces)]
    pltpu.make_async_copy(mine_w, mine_w, w_recv.at[0]).wait()
    pair_w = pltpu.make_async_remote_copy(
        src_ref=mine_w, dst_ref=mine_w, send_sem=w_send.at[1], recv_sem=w_recv.at[1],
        device_id={"member": sibling}, device_id_type=MESH,
    )
    pair_w.start()

    group = 8

    def rank(chunk):
        own_values(chunk).wait()
        rest = got.at[chunk, 0 : members_n - 1]
        pltpu.make_async_copy(rest, rest, a2a_recv.at[chunk]).wait()
        channel_half, at = place(me, chunk)
        area_row = area_ref[:, at] * (1.0 / count)

        def lay_out(source, _):
            for c in range(half_chan):
                flat[source, c * own_m : (c + 1) * own_m, :] = got[chunk, source, c]
            return 0

        lax.fori_loop(0, members_n, lay_out, 0)

        def rank_rows(tile, _):
            eight = pl.ds(pl.multiple_of(tile * 8, 8), 8)

            def value(k):
                start = pl.multiple_of(tile * 8 * own_m, 8) + k % own_m
                return flat[k // own_m, pl.ds(start, 8, stride=own_m), :]

            for one in range(0, count, group):
                left = [value(one + i) for i in range(group)]
                for other in range(one, count, group):
                    right = left if other == one else [value(other + i) for i in range(group)]
                    up = [None] * group
                    down = [None] * group
                    for i in range(group):
                        for j in range(i + 1 if other == one else 0, group):
                            above = jnp.where(left[i] > right[j], 1.0, 0.0)
                            up[i] = above if up[i] is None else up[i] + above
                            down[j] = above if down[j] is None else down[j] + above
                    for i in range(group):
                        if other == one:
                            less = float(i)
                            if up[i] is not None:
                                less = less + up[i]
                            if down[i] is not None:
                                less = less - down[i]
                            grads[one + i, eight, :] = less if one == 0 else grads[one + i, eight, :] + less
                        else:
                            grads[one + i, eight, :] += up[i]
                            below = float(group) - down[i]
                            grads[other + i, eight, :] = below if one == 0 else grads[other + i, eight, :] + below
            target = tgt[channel_half, eight, at]
            for k in range(count):
                grad = jnp.where(value(k) > target, float(2 * (count - 1)), 0.0) - 2.0 * grads[k, eight, :]
                grads[k, eight, :] = grad * area_row
            return 0

        lax.fori_loop(0, HALF_ROWS // 8, rank_rows, 0)

        def pack(k, _):
            back[chunk, k] = grads[k].astype(BF16)
            return 0

        lax.fori_loop(0, count, pack, 0)
        for k in range(1, members_n):
            grads_to(k, chunk).start()
        own_grads(chunk).start()

    def grads_place(chunk):
        channel_half, at = place(me, chunk)
        return og.at[:, pl.ds(pl.multiple_of(channel_half * HALF_ROWS, HALF_ROWS), HALF_ROWS), at]

    def grads_to(k, chunk):
        peer = member_peer(k)
        return pltpu.make_async_remote_copy(
            src_ref=back.at[chunk, pl.ds(peer * own_m, own_m)],
            dst_ref=grads_place(chunk),
            send_sem=back_send.at[chunk],
            recv_sem=back_recv.at[chunk],
            device_id={"member": peer},
            device_id_type=MESH,
        )

    def own_grads(chunk):
        return pltpu.make_async_copy(
            back.at[chunk, pl.ds(me * own_m, own_m)], grads_place(chunk), back_own.at[chunk]
        )

    def wait_grads(chunk):
        own_grads(chunk).wait()
        rest = back.at[chunk, 0 : count - own_m]
        pltpu.make_async_copy(rest, rest, back_recv.at[chunk]).wait()

    rank(0)

    pair_w.wait_recv()

    def weights():
        return wall[...].reshape(hid, wide + LANES)

    wt[...] = weights()[:, 0:wide].T

    nb = min(512, half_cells)

    def forward(chunk):
        def step(m, _):
            for b in range(0, half_cells, nb):
                at = slice(chunk * half_cells + b, chunk * half_cells + b + nb)
                bias2 = jnp.concatenate([bias_b[...]] * (nb // LANES), axis=1)
                v = dot_nn(wt[...], x[m, :, at]) + bias2
                sq = v * v
                u = 0.5 + 0.5 * jnp.tanh(v * (ROOT + (ROOT * CUBIC) * sq))
                a = v * u
                act[m, :, at] = a.astype(BF16)
                slope[m, :, at] = (u + a * (1.0 - u) * (2.0 * ROOT + (6.0 * ROOT * CUBIC) * sq)).astype(BF16)
            return 0

        lax.fori_loop(0, own_m, step, 0)

    for load in loads:
        load.wait()
    forward(0)
    forward(1)
    rank(1)

    def cut(chunk):
        return slice(chunk * half_cells, (chunk + 1) * half_cells)

    def pre_grads(chunk):
        at = cut(chunk)
        wop = weights()[:, wide:]

        def step(m, _):
            p = dot_nn(wop, og[m, :, at]) * slope[m, :, at].astype(F32)
            pg[m, :, at] = p.astype(BF16)
            folded = p[:, 0:LANES]
            for c in range(1, half_cells // LANES):
                folded = folded + p[:, c * LANES : (c + 1) * LANES]
            acc_b[...] += folded
            return 0

        lax.fori_loop(0, own_m, step, 0)

    def weight_terms(chunk, of):
        at = cut(chunk)

        def step(m, _):
            acc_in[of, :] += dot_nt(x[m, of, at], pg[m, :, at])
            acc_out[of, :] += dot_nt(act[m, of, at], og[m, :, at])
            return 0

        lax.fori_loop(0, own_m, step, 0)

    def input_grads(chunk):
        at = cut(chunk)

        def step(m, _):
            ig[m, :, at] = dot_nn(weights()[:, 0:wide], pg[m, :, at]).astype(BF16)
            return 0

        lax.fori_loop(0, own_m, step, 0)

    mine = pl.ds(pl.multiple_of(my_half * half_hid, half_hid), half_hid)
    theirs = pl.ds(pl.multiple_of((1 - my_half) * half_hid, half_hid), half_hid)

    wait_grads(0)
    pre_grads(0)
    weight_terms(0, slice(0, hid))
    input_grads(0)
    wait_grads(1)
    pre_grads(1)
    weight_terms(1, theirs)

    last_lane = lax.broadcasted_iota(jnp.int32, (half_hid, LANES), 1) == LANES - 1

    def out_terms(of):
        return jnp.where(last_lane, jnp.sum(acc_b[of, :], axis=1, keepdims=True), acc_out[of, :])

    part[:, 0:wide] = acc_in[theirs, :].astype(BF16)
    part[:, wide:] = out_terms(theirs).astype(BF16)
    to_sibling = pltpu.make_async_remote_copy(
        src_ref=part, dst_ref=pair, send_sem=pair_sem.at[0], recv_sem=pair_sem.at[1],
        device_id={"member": sibling}, device_id_type=MESH,
    )
    to_sibling.start()
    weight_terms(1, mine)
    to_sibling.wait_recv()
    total[:, 0:wide] = (acc_in[mine, :] + pair[:, 0:wide].astype(F32)).astype(BF16)
    total[:, wide:] = (out_terms(mine) + pair[:, wide:].astype(F32)).astype(BF16)

    slot = lax.rem(here, half_spaces)

    def send_block(k, _):
        block = lax.rem(here + k, half_spaces)
        pltpu.make_async_remote_copy(
            src_ref=total.at[pl.ds(pl.multiple_of(block * rows, rows), rows), :],
            dst_ref=shares.at[slot],
            send_sem=red_send, recv_sem=red_recv,
            device_id={"space": space_peer(k)}, device_id_type=MESH,
        ).start()
        return 0

    lax.fori_loop(first, half_spaces, send_block, 0)

    @pl.when(core == 0)
    def _():
        pltpu.make_async_copy(
            total.at[pl.ds(pl.multiple_of(slot * rows, rows), rows), :], shares.at[slot], red_recv
        ).start()

    input_grads(1)

    pltpu.make_async_copy(shares, shares, red_recv).wait()
    value = shares[0].astype(F32)
    for k in range(1, half_spaces):
        value = value + shares[k].astype(F32)
    owned[me] = value.astype(BF16)

    for k in range(1, members_n):
        pltpu.make_async_remote_copy(
            src_ref=owned.at[me], dst_ref=owned.at[me], send_sem=fin_send, recv_sem=fin_recv,
            device_id={"member": member_peer(k)}, device_id_type=MESH,
        ).start()
    rest = owned.at[0 : members_n - 1]
    pltpu.make_async_copy(rest, rest, fin_recv).wait()
    result = owned[0].astype(F32)
    for k in range(1, members_n):
        result = result + owned[k].astype(F32)
    result_out[...] = result * scale

    for chunk in range(2):
        rest = got.at[chunk, 0 : members_n - 1]
        pltpu.make_async_copy(rest, rest, a2a_send.at[chunk]).wait()
        rest = back.at[chunk, 0 : count - own_m]
        pltpu.make_async_copy(rest, rest, back_send.at[chunk]).wait()
    pair_w.wait_send()
    to_sibling.wait_send()
    rest = owned.at[0 : members_n - 1]
    pltpu.make_async_copy(rest, rest, fin_send).wait()

    def wait_sent(peers):
        rest = wall.at[0:peers]
        pltpu.make_async_copy(rest, rest, w_send.at[0]).wait()
        rest = shares.at[0:peers]
        pltpu.make_async_copy(rest, rest, red_send).wait()

    @pl.when(core == 0)
    def _():
        wait_sent(half_spaces - 1)

    @pl.when(core == 1)
    def _():
        wait_sent(half_spaces)


def body(members_n, spaces_n, inputs, w_in, bias_in, w_out, members_out, target, cell_area):
    own_m, hid, cells = inputs.shape
    rows, chan = w_out.shape
    wide = w_in.shape[1]
    count = own_m * members_n
    scale = 1.0 / math.sqrt(count * cells * spaces_n)
    half_chan = (chan + 1) // 2
    half_spaces = spaces_n // 2
    hbm_spec = pl.BlockSpec(memory_space=pltpu.HBM)
    vmem_spec = pl.BlockSpec(memory_space=pltpu.VMEM)
    dma = pltpu.SemaphoreType.DMA
    hidden = (own_m, hid, cells)
    full = wide + LANES
    operands = (
        inputs, w_in, bias_in.reshape(1, -1), w_out, members_out.transpose(1, 0, 2), target,
        cell_area.reshape(1, -1),
    )
    input_grad, result = pl.pallas_call(
        functools.partial(kernel, members_n, spaces_n, chan, scale),
        out_shape=(pltpu.VMEM(hidden, BF16), jax.ShapeDtypeStruct((rows, full), F32)),
        in_specs=[hbm_spec] * 7,
        out_specs=(vmem_spec, vmem_spec),
        scratch_shapes=[
            pltpu.VMEM(hidden, BF16),
            pltpu.VMEM((1, hid), F32),
            pltpu.VMEM((1, cells), F32),
            pltpu.VMEM((rows, full), BF16),
            pltpu.VMEM((rows, chan), BF16),
            pltpu.VMEM((rows, LANES), F32),
            pltpu.VMEM((spaces_n, rows, full), BF16),
            pltpu.VMEM((wide, hid), BF16),
            pltpu.VMEM((hid, LANES), F32),
            pltpu.VMEM((2, members_n, half_chan, own_m, LANES), F32),
            pltpu.VMEM((members_n, HALF_ROWS * own_m, LANES), F32),
            pltpu.VMEM((chan, cells), F32),
            pltpu.VMEM((2, HALF_ROWS, cells), F32),
            pltpu.VMEM((count, HALF_ROWS, LANES), F32),
            pltpu.VMEM((2, count, HALF_ROWS, LANES), BF16),
            pltpu.VMEM((own_m, LANES, cells), BF16),
            pltpu.VMEM(hidden, BF16),
            pltpu.VMEM(hidden, BF16),
            pltpu.VMEM(hidden, BF16),
            pltpu.VMEM((hid, wide), F32),
            pltpu.VMEM((hid, LANES), F32),
            pltpu.VMEM((hid, LANES), F32),
            pltpu.VMEM((hid // 2, full), BF16),
            pltpu.VMEM((hid // 2, full), BF16),
            pltpu.VMEM((hid // 2, full), BF16),
            pltpu.VMEM((half_spaces, rows, full), BF16),
            pltpu.VMEM((members_n, rows, full), BF16),
            dma((own_m + 5,)),
            dma((2,)),
            dma((2,)),
            dma((2,)),
            dma((2,)),
            dma((2,)),
            dma((2,)),
            dma((2,)),
            dma((2,)),
            dma((2,)),
            dma,
            dma,
            dma,
            dma,
        ],
        compiler_params=pltpu.CompilerParams(
            collective_id=0, has_side_effects=True, vmem_limit_bytes=48 * 1024 * 1024
        ),
        name="crps_backward",
    )(*(pltpu.with_memory_space_constraint(operand, pltpu.HBM) for operand in operands))
    second = wide + HALF_ROWS + 2 * half_chan - chan
    w_out_grad = jnp.concatenate(
        [result[:, wide : wide + half_chan], result[:, second : second + chan - half_chan]], axis=1
    )
    return input_grad, result[:, 0:wide], w_out_grad, result[:, full - 1]


def solution(mesh):
    members_n, spaces_n = mesh.shape["member"], mesh.shape["space"]
    return jax.shard_map(
        functools.partial(body, members_n, spaces_n),
        mesh=mesh,
        in_specs=(
            P("member", None, "space"),
            P("space", None),
            P(),
            P("space", None),
            P("member", None, "space"),
            P(None, "space"),
            P("space"),
        ),
        out_specs=(P("member", None, "space"), P("space", None), P("space", None), P("space")),
        check_vma=False,
    )
```

time: 636 us -> 62.2 us (0.10)
  waiting for transfers between devices: 346 us -> 0 us
  blocking collectives: 186 us -> 0 us
  Pallas kernels: 0 us -> 57.3 us
  matrix products: 31.8 us -> 0 us
  other arithmetic: 29 us -> 0.67 us
  local copies, waits for them, and re-layouts: 19.9 us -> 3.4 us
  between operations: 14.9 us -> 0.64 us
    reduce_scatter x1 -> x0, waiting for transfers between devices: 194 us -> none  [body(): lax.psum_scatter(term_out.astype(jnp.bfloat16), 'space', scatter_dimensio...]
    unnamed x3 -> x0, waiting for transfers between devices: 152 us -> none
    all_gather x2 -> x0, blocking collectives: 72 us -> none  [the longest x1 40.5 us: body(): lax.all_gather(w_in, 'space', axis=0, tiled=True)]
    pallas_call x0 -> x1, Pallas kernels: none -> 57.3 us  [body(): pl.pallas_call(functools.partial(kernel, members_n, spaces_n, chan, scale...]
    unnamed x1 -> x0, blocking collectives: 54.3 us -> none
    dot_general x5 -> x0, matrix products: 31.8 us -> none  [the longest x1 8.84 us: body(): jnp.einsum('oc,mcn->mon', w_out_all, out_grad, preferred_element_type=jnp...]
    all_to_all x1 -> x0, blocking collectives: 31.4 us -> none  [body(): lax.all_to_all(members_out, 'member', split_axis=2, concat_axis=0, tiled=...]
    psum x1 -> x0, blocking collectives: 28.1 us -> none  [body(): lax.psum(shares[0].astype(jnp.bfloat16), 'member').astype(jnp.float32)]
  transfers between devices with their start and end apart: 3 -> 0, of which waited for: 2 -> 0; matrix products, arithmetic and copies ran while one was open for 4% -> 0% of each run, Pallas kernels for 0% -> 0%
where the time goes in v2:
time: 62.2 us; the launch traced here: 62.1 us
  Pallas kernels  57.3 us (92%)
  local copies, waits for them, and re-layouts  3.4 us (5%)
  other arithmetic  0.67 us (1%)
  between operations  0.64 us (1%)
    pallas_call x1, Pallas kernels, body(): pl.pallas_call(functools.partial(kernel, members_n, spaces_n, chan, scale...  57.3 us
    unnamed x1, local copies, waits for them, and re-layouts  2.02 us
    slice x2, local copies, waits for them, and re-layouts, body(): return (input_grad, result[:, 0:wide], w_out_grad, result[:, full - 1])  1.31 us

profile of v2, /device:TPU:33, one launch (start us, length us, event | category | flops | bytes accessed | tf_op | source)
XLA Modules:
  0.0 62.1 jit_solution(11926034724510854406)
XLA Ops:
  0.6 57.3 %crps_backward.1 = (bf16[4,512,1024]{2,1,0:T(8,128)(2,1)S(1)}, f32[16,640]{1,0:T(8,128)S(1)}) custom-call(bf16[4,512,1024]{2,1,0:T(8,128)(2,1)} %x_hbm.1, bf16[16,512]{1,0:T(8,128)(2,1)} %w_hbm.1, f32[1,512]{1,0:T(1,128)} %bitcast.5, bf16[16,87]{1,0:T(8,128)(2,1)} %wo_hbm.1, f32[87,4,1024]{2,1,0:T(4,128)} %bitcast.3, f32[87,1024]{1,0:T(8,128)} %tgt_hbm.1, ...), custom_call_target="tpu_custom_call" | custom-call | tf_op jit(solution)/shard_map/crps_backward/pallas_call | solution.py:428
  58.0 2.0 %copy.12 = bf16[4,512,1024]{2,1,0:T(8,128)(2,1)} copy(bf16[4,512,1024]{2,1,0:T(8,128)(2,1)S(1)} %get-tuple-element.8) | data formatting | bytes 8388608
  60.0 0.7 %slice_reduce_fusion = f32[16]{0:T(128)} fusion(f32[16,640]{1,0:T(8,128)S(1)} %get-tuple-element.7), kind=kLoop, calls=%fused_computation.1 | loop fusion | bytes 128 | tf_op jit(solution)/shard_map/slice | solution.py:485
  60.7 0.1 slice.14
  60.8 0.6 slice.12
  61.4 0.7 %pad_maximum_fusion = f32[16,87]{1,0:T(8,128)} fusion(f32[16,43]{1,0:T(8,128)S(1)} %slice.14, f32[16,44]{1,0:T(8,128)S(1)} %slice.13), kind=kLoop, calls=%fused_computation | loop fusion | flops 1392 | bytes 11136 | tf_op jit(solution)/shard_map/concatenate | solution.py:482
  (1 shorter events, 0.0 us)

commit v3 on v2

--- a/solution.py
+++ b/solution.py
@@ -25,12 +25,18 @@
     return lax.dot_general(a, b, (((1,), (1,)), ((), ())), preferred_element_type=F32)
 
 
+def power(exponent):
+    near = jnp.exp2(exponent)
+    spread = near * float(2**16 + 1)
+    return spread - (spread - near)
+
+
 def kernel(
-    members_n, spaces_n, chan, scale,
+    members_n, spaces_n, chan,
     x_hbm, w_hbm, bias_hbm, wo_hbm, mem_hbm, tgt_hbm, area_hbm,
-    ig, result_out,
-    x, bias_ref, area_ref, stage, wo_raw, wo_wide, wall, wt, bias_b, got, flat, tgt_raw, tgt, grads, back, og, act, slope, pg,
-    acc_in, acc_out, acc_b, part, pair, total, shares, owned,
+    ig, owned,
+    x, bias_ref, area_ref, stage, wo_raw, wo_wide, wall, wt, bias_b, mem, flat, packed, got, values,
+    tgt_raw, tgt, grads, back, og, act, slope, pg, acc_in, acc_out, acc_b, part, pair, total, shares,
     load_sem, w_recv, w_send, a2a_recv, a2a_send, a2a_own, back_recv, back_send, back_own,
     pair_sem, red_recv, red_send, fin_recv, fin_send,
 ):
@@ -45,7 +51,8 @@
     half_cells = cells // 2
     count = own_m * members_n
     wide = wt.shape[0]
-    half_chan = got.shape[2]
+    half_chan = (chan + 1) // 2
+    words = own_m - 1
     my_half = lax.rem(here // half_spaces + core, 2)
     sibling = me + 1 - 2 * core
 
@@ -75,6 +82,14 @@
     load_bias = pltpu.make_async_copy(bias_hbm, bias_ref, load_sem.at[own_m + 3])
     load_area = pltpu.make_async_copy(area_hbm, area_ref, load_sem.at[own_m + 4])
     loads = [pltpu.make_async_copy(x_hbm.at[m], x.at[m], load_sem.at[m]) for m in range(own_m)]
+    load_mem = [
+        pltpu.make_async_copy(
+            mem_hbm.at[:, :, t * LANES : (t + 1) * LANES], mem.at[t], load_sem.at[own_m + 5 + t]
+        )
+        for t in range(members_n)
+    ]
+    for load in load_mem:
+        load.start()
     load_w.start()
     load_wo.start()
     load_tgt.start()
@@ -91,21 +106,59 @@
     stage[:, wide:] = wo_wide[...].astype(BF16)
     load_w.wait()
 
-    pl.semaphore_wait(barrier, members_n - 1 + half_spaces - first)
-
     def place(peer, chunk):
         channel_half = lax.rem(peer // half_members + chunk, 2)
         tile = lax.rem(peer, half_members) + chunk * half_members
         return channel_half, pl.ds(pl.multiple_of(tile * LANES, LANES), LANES)
 
-    def values_from(peer, chunk):
-        channel_half, at = place(peer, chunk)
-        return mem_hbm.at[pl.ds(channel_half * (chan - half_chan), half_chan), :, at]
+    flat[half_chan * own_m :, :] = jnp.zeros((flat.shape[0] - half_chan * own_m, LANES), F32)
+
+    def encode(chunk):
+        def step(peer, _):
+            channel_half, _ = place(peer, chunk)
+            tile = lax.rem(peer, half_members) + chunk * half_members
+            start = channel_half * (chan - half_chan)
+            for c in range(half_chan):
+                flat[c * own_m : (c + 1) * own_m, :] = mem[tile, start + c]
+            for i in reversed(range(HALF_ROWS // 8)):
+                whole = [
+                    flat[pl.ds(i * 8 * own_m + m, 8, stride=own_m), :] * float(2**18) for m in range(own_m)
+                ]
+                code = whole[words] - float(2**21)
+                size = jnp.abs(code)
+                digit2 = jnp.floor(size * (1.0 / 2**14))
+                size = size - digit2 * float(2**14)
+                digit1 = jnp.floor(size * (1.0 / 2**7))
+                digits = (size - digit1 * float(2**7), digit1, digit2)
+                for j in range(words):
+                    word = (whole[j] + float(2**23)) * power(digits[j] - 64.0)
+                    if j == words - 1:
+                        word = jnp.where(code < 0.0, -word, word)
+                    packed[chunk, peer, j * half_chan + i * 8 : j * half_chan + (i + 1) * 8, :] = word
+            return 0
+
+        lax.fori_loop(0, members_n, step, 0)
+
+    def decode(chunk):
+        def step(source, _):
+            for i in range(HALF_ROWS // 8):
+                rank_rows = slice(i * 8, (i + 1) * 8)
+                digits = [None] * words
+                for j in range(words):
+                    word = got[chunk, source, j * half_chan + i * 8 : j * half_chan + (i + 1) * 8, :]
+                    size = jnp.abs(word) if j == words - 1 else word
+                    digits[j] = jnp.floor(jnp.log2(size) + 0.2) + (64.0 - 23.0)
+                    values[source * own_m + j, rank_rows, :] = size * power(64.0 - digits[j]) - float(2**23)
+                code = (digits[2] * 128.0 + digits[1]) * 128.0 + digits[0]
+                values[source * own_m + words, rank_rows, :] = jnp.where(word < 0.0, -code, code) + float(2**21)
+            return 0
+
+        lax.fori_loop(0, members_n, step, 0)
 
     def values_to(k, chunk):
         peer = member_peer(k)
         return pltpu.make_async_remote_copy(
-            src_ref=values_from(peer, chunk),
+            src_ref=packed.at[chunk, peer],
             dst_ref=got.at[chunk, me],
             send_sem=a2a_send.at[chunk],
             recv_sem=a2a_recv.at[chunk],
@@ -114,12 +167,16 @@
         )
 
     def own_values(chunk):
-        return pltpu.make_async_copy(values_from(me, chunk), got.at[chunk, me], a2a_own.at[chunk])
+        return pltpu.make_async_copy(packed.at[chunk, me], got.at[chunk, me], a2a_own.at[chunk])
 
     def send_values(chunk):
         for k in range(1, members_n):
             values_to(k, chunk).start()
         own_values(chunk).start()
+
+    def values_sent(chunk):
+        rest = got.at[chunk, 0 : members_n - 1]
+        pltpu.make_async_copy(rest, rest, a2a_send.at[chunk]).wait()
 
     def send_rows(k, _):
         pltpu.make_async_remote_copy(
@@ -128,6 +185,11 @@
         ).start()
         return 0
 
+    for load in load_mem:
+        load.wait()
+    encode(0)
+    encode(1)
+    pl.semaphore_wait(barrier, members_n - 1 + half_spaces - first)
     send_values(0)
     lax.fori_loop(first, half_spaces, send_rows, 0)
 
@@ -141,14 +203,13 @@
     load_area.wait()
     bias_b[...] = jnp.broadcast_to(bias_ref[...], (LANES, hid)).T
     og[:, 2 * HALF_ROWS :, :] = jnp.zeros((own_m, og.shape[1] - 2 * HALF_ROWS, cells), BF16)
-    flat[...] = jnp.zeros(flat.shape, F32)
     tgt[...] = jnp.zeros(tgt.shape, F32)
     acc_in[...] = jnp.zeros(acc_in.shape, F32)
     acc_out[...] = jnp.zeros(acc_out.shape, F32)
     acc_b[...] = jnp.zeros(acc_b.shape, F32)
     load_tgt.wait()
-    tgt[0, 0:half_chan, :] = tgt_raw[0:half_chan, :]
-    tgt[1, 0:half_chan, :] = tgt_raw[chan - half_chan : chan, :]
+    tgt[0, 0:half_chan, :] = tgt_raw[0:half_chan, :] * float(2**18)
+    tgt[1, 0:half_chan, :] = tgt_raw[chan - half_chan : chan, :] * float(2**18)
 
     mine_w = wall.at[pl.ds(my_half * half_spaces, half_spaces)]
     pltpu.make_async_copy(mine_w, mine_w, w_recv.at[0]).wait()
@@ -167,19 +228,13 @@
         channel_half, at = place(me, chunk)
         area_row = area_ref[:, at] * (1.0 / count)
 
-        def lay_out(source, _):
-            for c in range(half_chan):
-                flat[source, c * own_m : (c + 1) * own_m, :] = got[chunk, source, c]
-            return 0
-
-        lax.fori_loop(0, members_n, lay_out, 0)
+        decode(chunk)
 
         def rank_rows(tile, _):
             eight = pl.ds(pl.multiple_of(tile * 8, 8), 8)
 
             def value(k):
-                start = pl.multiple_of(tile * 8 * own_m, 8) + k % own_m
-                return flat[k // own_m, pl.ds(start, 8, stride=own_m), :]
+                return values[k, eight, :]
 
             for one in range(0, count, group):
                 left = [value(one + i) for i in range(group)]
@@ -217,6 +272,8 @@
             return 0
 
         lax.fori_loop(0, count, pack, 0)
+
+    def send_grads(chunk):
         for k in range(1, members_n):
             grads_to(k, chunk).start()
         own_grads(chunk).start()
@@ -247,6 +304,8 @@
         pltpu.make_async_copy(rest, rest, back_recv.at[chunk]).wait()
 
     rank(0)
+    values_sent(1)
+    send_grads(0)
 
     pair_w.wait_recv()
 
@@ -275,8 +334,9 @@
     for load in loads:
         load.wait()
     forward(0)
+    rank(1)
+    send_grads(1)
     forward(1)
-    rank(1)
 
     def cut(chunk):
         return slice(chunk * half_cells, (chunk + 1) * half_cells)
@@ -321,7 +381,6 @@
     wait_grads(0)
     pre_grads(0)
     weight_terms(0, slice(0, hid))
-    input_grads(0)
     wait_grads(1)
     pre_grads(1)
     weight_terms(1, theirs)
@@ -363,6 +422,7 @@
             total.at[pl.ds(pl.multiple_of(slot * rows, rows), rows), :], shares.at[slot], red_recv
         ).start()
 
+    input_grads(0)
     input_grads(1)
 
     pltpu.make_async_copy(shares, shares, red_recv).wait()
@@ -378,14 +438,8 @@
         ).start()
     rest = owned.at[0 : members_n - 1]
     pltpu.make_async_copy(rest, rest, fin_recv).wait()
-    result = owned[0].astype(F32)
-    for k in range(1, members_n):
-        result = result + owned[k].astype(F32)
-    result_out[...] = result * scale
-
+    values_sent(0)
     for chunk in range(2):
-        rest = got.at[chunk, 0 : members_n - 1]
-        pltpu.make_async_copy(rest, rest, a2a_send.at[chunk]).wait()
         rest = back.at[chunk, 0 : count - own_m]
         pltpu.make_async_copy(rest, rest, back_send.at[chunk]).wait()
     pair_w.wait_send()
@@ -406,6 +460,35 @@
     @pl.when(core == 1)
     def _():
         wait_sent(half_spaces)
+
+
+def finish(
+    chan, scale, ig_ref, owned_ref, ig_out, win_out, wout_out, bias_out, win, wout, bias, sem
+):
+    copies = [pltpu.make_async_copy(ig_ref.at[m], ig_out.at[m], sem.at[m]) for m in range(ig_ref.shape[0])]
+    for copy in copies:
+        copy.start()
+    members_n, rows, full = owned_ref.shape
+    wide = full - LANES
+    half_chan = (chan + 1) // 2
+    result = owned_ref[0].astype(F32)
+    for k in range(1, members_n):
+        result = result + owned_ref[k].astype(F32)
+    result = result * scale
+    win[...] = result[:, 0:wide]
+    wout[:, 0:half_chan] = result[:, wide : wide + half_chan]
+    second = wide + HALF_ROWS + 2 * half_chan - chan
+    wout[:, half_chan:chan] = result[:, second : second + chan - half_chan]
+    diagonal = lax.broadcasted_iota(jnp.int32, (rows, rows), 0) == lax.broadcasted_iota(
+        jnp.int32, (rows, rows), 1
+    )
+    bias[...] = jnp.sum(jnp.where(diagonal, result[:, full - 1 : full], 0.0), axis=0, keepdims=True)
+    first = len(copies)
+    for k, (source, out) in enumerate(((win, win_out), (wout, wout_out), (bias, bias_out))):
+        copies.append(pltpu.make_async_copy(source, out, sem.at[first + k]))
+        copies[-1].start()
+    for copy in copies:
+        copy.wait()
 
 
 def body(members_n, spaces_n, inputs, w_in, bias_in, w_out, members_out, target, cell_area):
@@ -415,6 +498,7 @@
     count = own_m * members_n
     scale = 1.0 / math.sqrt(count * cells * spaces_n)
     half_chan = (chan + 1) // 2
+    packed_rows = (own_m - 2) * half_chan + HALF_ROWS
     half_spaces = spaces_n // 2
     hbm_spec = pl.BlockSpec(memory_space=pltpu.HBM)
     vmem_spec = pl.BlockSpec(memory_space=pltpu.VMEM)
@@ -425,9 +509,9 @@
         inputs, w_in, bias_in.reshape(1, -1), w_out, members_out.transpose(1, 0, 2), target,
         cell_area.reshape(1, -1),
     )
-    input_grad, result = pl.pallas_call(
-        functools.partial(kernel, members_n, spaces_n, chan, scale),
-        out_shape=(pltpu.VMEM(hidden, BF16), jax.ShapeDtypeStruct((rows, full), F32)),
+    partial = pl.pallas_call(
+        functools.partial(kernel, members_n, spaces_n, chan),
+        out_shape=(pltpu.VMEM(hidden, BF16), pltpu.VMEM((members_n, rows, full), BF16)),
         in_specs=[hbm_spec] * 7,
         out_specs=(vmem_spec, vmem_spec),
         scratch_shapes=[
@@ -440,8 +524,11 @@
             pltpu.VMEM((spaces_n, rows, full), BF16),
             pltpu.VMEM((wide, hid), BF16),
             pltpu.VMEM((hid, LANES), F32),
-            pltpu.VMEM((2, members_n, half_chan, own_m, LANES), F32),
-            pltpu.VMEM((members_n, HALF_ROWS * own_m, LANES), F32),
+            pltpu.VMEM((members_n, chan, own_m, LANES), F32),
+            pltpu.VMEM((HALF_ROWS * own_m, LANES), F32),
+            pltpu.VMEM((2, members_n, packed_rows, LANES), F32),
+            pltpu.VMEM((2, members_n, packed_rows, LANES), F32),
+            pltpu.VMEM((count, HALF_ROWS, LANES), F32),
             pltpu.VMEM((chan, cells), F32),
             pltpu.VMEM((2, HALF_ROWS, cells), F32),
             pltpu.VMEM((count, HALF_ROWS, LANES), F32),
@@ -457,8 +544,7 @@
             pltpu.VMEM((hid // 2, full), BF16),
             pltpu.VMEM((hid // 2, full), BF16),
             pltpu.VMEM((half_spaces, rows, full), BF16),
-            pltpu.VMEM((members_n, rows, full), BF16),
-            dma((own_m + 5,)),
+            dma((own_m + 5 + members_n,)),
             dma((2,)),
             dma((2,)),
             dma((2,)),
@@ -478,11 +564,26 @@
         ),
         name="crps_backward",
     )(*(pltpu.with_memory_space_constraint(operand, pltpu.HBM) for operand in operands))
-    second = wide + HALF_ROWS + 2 * half_chan - chan
-    w_out_grad = jnp.concatenate(
-        [result[:, wide : wide + half_chan], result[:, second : second + chan - half_chan]], axis=1
-    )
-    return input_grad, result[:, 0:wide], w_out_grad, result[:, full - 1]
+    input_grad, w_in_grad, w_out_grad, bias_grad = pl.pallas_call(
+        functools.partial(finish, chan, scale),
+        out_shape=(
+            jax.ShapeDtypeStruct(hidden, BF16),
+            jax.ShapeDtypeStruct((rows, wide), F32),
+            jax.ShapeDtypeStruct((rows, chan), F32),
+            jax.ShapeDtypeStruct((1, rows), F32),
+        ),
+        in_specs=[vmem_spec, vmem_spec],
+        out_specs=(hbm_spec,) * 4,
+        scratch_shapes=[
+            pltpu.VMEM((rows, wide), F32),
+            pltpu.VMEM((rows, chan), F32),
+            pltpu.VMEM((1, rows), F32),
+            dma((own_m + 3,)),
+        ],
+        compiler_params=pltpu.CompilerParams(vmem_limit_bytes=16 * 1024 * 1024),
+        name="finish",
+    )(*(pltpu.with_memory_space_constraint(array, pltpu.VMEM) for array in partial))
+    return input_grad, w_in_grad, w_out_grad, bias_grad.reshape(rows)
 
 
 def solution(mesh):

time: 62.2 us -> 59 us (0.949)
  local copies, waits for them, and re-layouts: 3.4 us -> 0 us
  Pallas kernels: 57.3 us -> 58.3 us
  other arithmetic: 0.67 us -> 0 us
    unnamed x1 -> x0, local copies, waits for them, and re-layouts: 2.02 us -> none
    slice x4 -> x0, local copies, waits for them, and re-layouts: 1.38 us -> none  [the longest x2 1.31 us: body(): return (input_grad, result[:, 0:wide], w_out_grad, result[:, full - 1])]
    pallas_call x1 -> x2, Pallas kernels: 57.3 us -> 58.3 us  [the longest x1 56.2 us: body(): pl.pallas_call(functools.partial(kernel, members_n, spaces_n, chan), out_...]
    concatenate x1 -> x0, other arithmetic: 0.67 us -> none  [body(): jnp.concatenate([result[:, wide:wide + half_chan], result[:, second:secon...]
where the time goes in v3:
time: 59 us; the launch traced here: 58.9 us
  Pallas kernels  58.3 us (99%)
  between operations  0.64 us (1%)
    pallas_call x1, Pallas kernels, body(): pl.pallas_call(functools.partial(kernel, members_n, spaces_n, chan), out_...  56.2 us
    pallas_call x1, Pallas kernels, body(): pl.pallas_call(functools.partial(finish, chan, scale), out_shape=(jax.Sha...  2.07 us

profile of v3, /device:TPU:33, one launch (start us, length us, event | category | flops | bytes accessed | tf_op | source)
XLA Modules:
  0.0 58.9 jit_solution(2027719857992675809)
XLA Ops:
  0.6 56.2 %crps_backward.1 = (bf16[4,512,1024]{2,1,0:T(8,128)(2,1)S(1)}, bf16[8,16,640]{2,1,0:T(8,128)(2,1)S(1)}) custom-call(bf16[4,512,1024]{2,1,0:T(8,128)(2,1)} %x_hbm.1, bf16[16,512]{1,0:T(8,128)(2,1)} %w_hbm.1, f32[1,512]{1,0:T(1,128)} %bitcast.6, bf16[16,87]{1,0:T(8,128)(2,1)} %wo_hbm.1, f32[87,4,1024]{2,1,0:T(4,128)} %bitcast.4, f32[87,1024]{1,0:T(8,128)} %tgt_hbm.1, ...), custom_call_target="tpu_custom_call" | custom-call | tf_op jit(solution)/shard_map/crps_backward/pallas_call | solution.py:512
  56.8 2.1 %finish.1 = (bf16[4,512,1024]{2,1,0:T(8,128)(2,1)}, f32[16,512]{1,0:T(8,128)}, f32[16,87]{1,0:T(8,128)}, f32[1,16]{1,0:T(1,128)}) custom-call(bf16[4,512,1024]{2,1,0:T(8,128)(2,1)S(1)} %get-tuple-element.10.ig_ref, bf16[8,16,640]{2,1,0:T(8,128)(2,1)S(1)} %get-tuple-element.11.owned_ref), custom_call_target="tpu_custom_call" | custom-call | tf_op jit(solution)/shard_map/finish/pallas_call | solution.py:567

commit v4 on v3

--- a/solution.py
+++ b/solution.py
@@ -62,6 +62,7 @@
     def space_peer(k):
         return my_half * half_spaces + lax.rem(here + k, half_spaces)
 
+    far_first = sorted(range(1, members_n), key=lambda k: -min(k, members_n - k))
     barrier = pltpu.get_barrier_semaphore()
 
     def greet_space(k, _):
@@ -170,7 +171,7 @@
         return pltpu.make_async_copy(packed.at[chunk, me], got.at[chunk, me], a2a_own.at[chunk])
 
     def send_values(chunk):
-        for k in range(1, members_n):
+        for k in far_first:
             values_to(k, chunk).start()
         own_values(chunk).start()
 
@@ -274,7 +275,7 @@
         lax.fori_loop(0, count, pack, 0)
 
     def send_grads(chunk):
-        for k in range(1, members_n):
+        for k in far_first:
             grads_to(k, chunk).start()
         own_grads(chunk).start()
 
@@ -329,7 +330,8 @@
                 slope[m, :, at] = (u + a * (1.0 - u) * (2.0 * ROOT + (6.0 * ROOT * CUBIC) * sq)).astype(BF16)
             return 0
 
-        lax.fori_loop(0, own_m, step, 0)
+        for m in range(own_m):
+            step(m, 0)
 
     for load in loads:
         load.wait()
@@ -354,17 +356,17 @@
             acc_b[...] += folded
             return 0
 
-        lax.fori_loop(0, own_m, step, 0)
+        for m in range(own_m):
+            step(m, 0)
 
     def weight_terms(chunk, of):
         at = cut(chunk)
-
-        def step(m, _):
-            acc_in[of, :] += dot_nt(x[m, of, at], pg[m, :, at])
-            acc_out[of, :] += dot_nt(act[m, of, at], og[m, :, at])
-            return 0
-
-        lax.fori_loop(0, own_m, step, 0)
+        acc_in[of, :] += functools.reduce(
+            jnp.add, [dot_nt(x[m, of, at], pg[m, :, at]) for m in range(own_m)]
+        )
+        acc_out[of, :] += functools.reduce(
+            jnp.add, [dot_nt(act[m, of, at], og[m, :, at]) for m in range(own_m)]
+        )
 
     def input_grads(chunk):
         at = cut(chunk)
@@ -431,7 +433,7 @@
         value = value + shares[k].astype(F32)
     owned[me] = value.astype(BF16)
 
-    for k in range(1, members_n):
+    for k in far_first:
         pltpu.make_async_remote_copy(
             src_ref=owned.at[me], dst_ref=owned.at[me], send_sem=fin_send, recv_sem=fin_recv,
             device_id={"member": member_peer(k)}, device_id_type=MESH,

time: 59 us -> 55 us (0.932)
  Pallas kernels: 58.3 us -> 54.2 us
    pallas_call x1, Pallas kernels: 56.2 us -> 52.1 us  [body(): pl.pallas_call(functools.partial(kernel, members_n, spaces_n, chan), out_...]
where the time goes in v4:
time: 55 us; the launch traced here: 54.8 us
  Pallas kernels  54.2 us (99%)
  between operations  0.64 us (1%)
    pallas_call x1, Pallas kernels, body(): pl.pallas_call(functools.partial(kernel, members_n, spaces_n, chan), out_...  52.1 us
    pallas_call x1, Pallas kernels, body(): pl.pallas_call(functools.partial(finish, chan, scale), out_shape=(jax.Sha...  2.07 us

profile of v4, /device:TPU:33, one launch (start us, length us, event | category | flops | bytes accessed | tf_op | source)
XLA Modules:
  0.0 54.8 jit_solution(5673752335275932451)
XLA Ops:
  0.6 52.1 %crps_backward.1 = (bf16[4,512,1024]{2,1,0:T(8,128)(2,1)S(1)}, bf16[8,16,640]{2,1,0:T(8,128)(2,1)S(1)}) custom-call(bf16[4,512,1024]{2,1,0:T(8,128)(2,1)} %x_hbm.1, bf16[16,512]{1,0:T(8,128)(2,1)} %w_hbm.1, f32[1,512]{1,0:T(1,128)} %bitcast.6, bf16[16,87]{1,0:T(8,128)(2,1)} %wo_hbm.1, f32[87,4,1024]{2,1,0:T(4,128)} %bitcast.4, f32[87,1024]{1,0:T(8,128)} %tgt_hbm.1, ...), custom_call_target="tpu_custom_call" | custom-call | tf_op jit(solution)/shard_map/crps_backward/pallas_call | solution.py:514
  52.7 2.1 %finish.1 = (bf16[4,512,1024]{2,1,0:T(8,128)(2,1)}, f32[16,512]{1,0:T(8,128)}, f32[16,87]{1,0:T(8,128)}, f32[1,16]{1,0:T(1,128)}) custom-call(bf16[4,512,1024]{2,1,0:T(8,128)(2,1)S(1)} %get-tuple-element.10.ig_ref, bf16[8,16,640]{2,1,0:T(8,128)(2,1)S(1)} %get-tuple-element.11.owned_ref), custom_call_target="tpu_custom_call" | custom-call | tf_op jit(solution)/shard_map/finish/pallas_call | solution.py:569

commit v5 on v4

--- a/solution.py
+++ b/solution.py
@@ -43,7 +43,7 @@
     me = lax.axis_index("member")
     here = lax.axis_index("space")
     core = lax.rem(me, 2)
-    own_m, hid, cells = x.shape
+    own_m, hid, cells = ig.shape
     rows = w_hbm.shape[0]
     half_spaces = spaces_n // 2
     half_members = members_n // 2
@@ -82,7 +82,20 @@
     load_tgt = pltpu.make_async_copy(tgt_hbm, tgt_raw, load_sem.at[own_m + 2])
     load_bias = pltpu.make_async_copy(bias_hbm, bias_ref, load_sem.at[own_m + 3])
     load_area = pltpu.make_async_copy(area_hbm, area_ref, load_sem.at[own_m + 4])
-    loads = [pltpu.make_async_copy(x_hbm.at[m], x.at[m], load_sem.at[m]) for m in range(own_m)]
+
+    def columns(chunk, m, members=1):
+        start = (chunk * own_m + m) * half_cells
+        return slice(start, start + members * half_cells)
+
+    loads = [
+        pltpu.make_async_copy(
+            x_hbm.at[m, :, chunk * half_cells : (chunk + 1) * half_cells],
+            x.at[:, columns(chunk, m)],
+            load_sem.at[m if chunk == 0 else own_m + 5 + members_n + m],
+        )
+        for chunk in range(2)
+        for m in range(own_m)
+    ]
     load_mem = [
         pltpu.make_async_copy(
             mem_hbm.at[:, :, t * LANES : (t + 1) * LANES], mem.at[t], load_sem.at[own_m + 5 + t]
@@ -192,21 +205,19 @@
     encode(1)
     pl.semaphore_wait(barrier, members_n - 1 + half_spaces - first)
     send_values(0)
+    send_values(1)
     lax.fori_loop(first, half_spaces, send_rows, 0)
 
     @pl.when(core == 0)
     def _():
         pltpu.make_async_copy(stage, wall.at[here], w_recv.at[0]).start()
 
-    send_values(1)
 
     load_bias.wait()
     load_area.wait()
     bias_b[...] = jnp.broadcast_to(bias_ref[...], (LANES, hid)).T
     og[:, 2 * HALF_ROWS :, :] = jnp.zeros((own_m, og.shape[1] - 2 * HALF_ROWS, cells), BF16)
     tgt[...] = jnp.zeros(tgt.shape, F32)
-    acc_in[...] = jnp.zeros(acc_in.shape, F32)
-    acc_out[...] = jnp.zeros(acc_out.shape, F32)
     acc_b[...] = jnp.zeros(acc_b.shape, F32)
     load_tgt.wait()
     tgt[0, 0:half_chan, :] = tgt_raw[0:half_chan, :] * float(2**18)
@@ -315,23 +326,20 @@
 
     wt[...] = weights()[:, 0:wide].T
 
-    nb = min(512, half_cells)
+    def cut(chunk):
+        return slice(chunk * half_cells, (chunk + 1) * half_cells)
+
 
     def forward(chunk):
-        def step(m, _):
-            for b in range(0, half_cells, nb):
-                at = slice(chunk * half_cells + b, chunk * half_cells + b + nb)
-                bias2 = jnp.concatenate([bias_b[...]] * (nb // LANES), axis=1)
-                v = dot_nn(wt[...], x[m, :, at]) + bias2
-                sq = v * v
-                u = 0.5 + 0.5 * jnp.tanh(v * (ROOT + (ROOT * CUBIC) * sq))
-                a = v * u
-                act[m, :, at] = a.astype(BF16)
-                slope[m, :, at] = (u + a * (1.0 - u) * (2.0 * ROOT + (6.0 * ROOT * CUBIC) * sq)).astype(BF16)
-            return 0
-
+        at = cut(chunk)
+        bias2 = jnp.concatenate([bias_b[...]] * (half_cells // LANES), axis=1)
         for m in range(own_m):
-            step(m, 0)
+            v = dot_nn(wt[...], x[:, columns(chunk, m)]) + bias2
+            sq = v * v
+            u = 0.5 + 0.5 * jnp.tanh(v * (ROOT + (ROOT * CUBIC) * sq))
+            a = v * u
+            act[m, :, at] = a.astype(BF16)
+            slope[m, :, at] = (u + a * (1.0 - u) * (2.0 * ROOT + (6.0 * ROOT * CUBIC) * sq)).astype(BF16)
 
     for load in loads:
         load.wait()
@@ -340,39 +348,31 @@
     send_grads(1)
     forward(1)
 
-    def cut(chunk):
-        return slice(chunk * half_cells, (chunk + 1) * half_cells)
-
     def pre_grads(chunk):
         at = cut(chunk)
         wop = weights()[:, wide:]
-
-        def step(m, _):
+        for m in range(own_m):
             p = dot_nn(wop, og[m, :, at]) * slope[m, :, at].astype(F32)
-            pg[m, :, at] = p.astype(BF16)
+            pg[:, columns(chunk, m)] = p.astype(BF16)
             folded = p[:, 0:LANES]
             for c in range(1, half_cells // LANES):
                 folded = folded + p[:, c * LANES : (c + 1) * LANES]
             acc_b[...] += folded
-            return 0
-
-        for m in range(own_m):
-            step(m, 0)
-
-    def weight_terms(chunk, of):
+
+    def terms_in(chunk, of):
+        every = columns(chunk, 0, own_m)
+        return dot_nt(x[of, every], pg[:, every])
+
+    def terms_out(chunk, of):
         at = cut(chunk)
-        acc_in[of, :] += functools.reduce(
-            jnp.add, [dot_nt(x[m, of, at], pg[m, :, at]) for m in range(own_m)]
-        )
-        acc_out[of, :] += functools.reduce(
-            jnp.add, [dot_nt(act[m, of, at], og[m, :, at]) for m in range(own_m)]
-        )
+        return functools.reduce(jnp.add, [dot_nt(act[m, of, at], og[m, :, at]) for m in range(own_m)])
 
     def input_grads(chunk):
         at = cut(chunk)
 
         def step(m, _):
-            ig[m, :, at] = dot_nn(weights()[:, 0:wide], pg[m, :, at]).astype(BF16)
+            start = pl.multiple_of((chunk * own_m + m) * half_cells, half_cells)
+            ig[m, :, at] = dot_nn(weights()[:, 0:wide], pg[:, pl.ds(start, half_cells)]).astype(BF16)
             return 0
 
         lax.fori_loop(0, own_m, step, 0)
@@ -382,27 +382,29 @@
 
     wait_grads(0)
     pre_grads(0)
-    weight_terms(0, slice(0, hid))
+    for of in (slice(0, half_hid), slice(half_hid, hid)):
+        acc_in[of, :] = terms_in(0, of)
+        acc_out[of, :] = terms_out(0, of)
     wait_grads(1)
     pre_grads(1)
-    weight_terms(1, theirs)
 
     last_lane = lax.broadcasted_iota(jnp.int32, (half_hid, LANES), 1) == LANES - 1
 
-    def out_terms(of):
-        return jnp.where(last_lane, jnp.sum(acc_b[of, :], axis=1, keepdims=True), acc_out[of, :])
-
-    part[:, 0:wide] = acc_in[theirs, :].astype(BF16)
-    part[:, wide:] = out_terms(theirs).astype(BF16)
+    def with_bias(of, terms):
+        return jnp.where(last_lane, jnp.sum(acc_b[of, :], axis=1, keepdims=True), terms)
+
+    part[:, 0:wide] = (acc_in[theirs, :] + terms_in(1, theirs)).astype(BF16)
+    part[:, wide:] = with_bias(theirs, acc_out[theirs, :] + terms_out(1, theirs)).astype(BF16)
     to_sibling = pltpu.make_async_remote_copy(
         src_ref=part, dst_ref=pair, send_sem=pair_sem.at[0], recv_sem=pair_sem.at[1],
         device_id={"member": sibling}, device_id_type=MESH,
     )
     to_sibling.start()
-    weight_terms(1, mine)
+    acc_in[mine, :] += terms_in(1, mine)
+    acc_out[mine, :] = with_bias(mine, acc_out[mine, :] + terms_out(1, mine))
     to_sibling.wait_recv()
     total[:, 0:wide] = (acc_in[mine, :] + pair[:, 0:wide].astype(F32)).astype(BF16)
-    total[:, wide:] = (out_terms(mine) + pair[:, wide:].astype(F32)).astype(BF16)
+    total[:, wide:] = (acc_out[mine, :] + pair[:, wide:].astype(F32)).astype(BF16)
 
     slot = lax.rem(here, half_spaces)
 
@@ -517,7 +519,7 @@
         in_specs=[hbm_spec] * 7,
         out_specs=(vmem_spec, vmem_spec),
         scratch_shapes=[
-            pltpu.VMEM(hidden, BF16),
+            pltpu.VMEM((hid, own_m * cells), BF16),
             pltpu.VMEM((1, hid), F32),
             pltpu.VMEM((1, cells), F32),
             pltpu.VMEM((rows, full), BF16),
@@ -538,7 +540,7 @@
             pltpu.VMEM((own_m, LANES, cells), BF16),
             pltpu.VMEM(hidden, BF16),
             pltpu.VMEM(hidden, BF16),
-            pltpu.VMEM(hidden, BF16),
+            pltpu.VMEM((hid, own_m * cells), BF16),
             pltpu.VMEM((hid, wide), F32),
             pltpu.VMEM((hid, LANES), F32),
             pltpu.VMEM((hid, LANES), F32),
@@ -546,7 +548,7 @@
             pltpu.VMEM((hid // 2, full), BF16),
             pltpu.VMEM((hid // 2, full), BF16),
             pltpu.VMEM((half_spaces, rows, full), BF16),
-            dma((own_m + 5 + members_n,)),
+            dma((2 * own_m + 5 + members_n,)),
             dma((2,)),
             dma((2,)),
             dma((2,)),

time: 55 us -> 55 us (level)
  no operation moved by 1% of the time
where the time goes in v5:
time: 55 us; the launch traced here: 54.6 us
  Pallas kernels  54 us (98%)
  between operations  0.64 us (1%)
    pallas_call x1, Pallas kernels, body(): pl.pallas_call(functools.partial(kernel, members_n, spaces_n, chan), out_...  51.9 us
    pallas_call x1, Pallas kernels, body(): pl.pallas_call(functools.partial(finish, chan, scale), out_shape=(jax.Sha...  2.07 us

profile of v5, /device:TPU:33, one launch (start us, length us, event | category | flops | bytes accessed | tf_op | source)
XLA Modules:
  0.0 54.6 jit_solution(16758362949147967378)
XLA Ops:
  0.6 51.9 %crps_backward.1 = (bf16[4,512,1024]{2,1,0:T(8,128)(2,1)S(1)}, bf16[8,16,640]{2,1,0:T(8,128)(2,1)S(1)}) custom-call(bf16[4,512,1024]{2,1,0:T(8,128)(2,1)} %x_hbm.1, bf16[16,512]{1,0:T(8,128)(2,1)} %w_hbm.1, f32[1,512]{1,0:T(1,128)} %bitcast.6, bf16[16,87]{1,0:T(8,128)(2,1)} %wo_hbm.1, f32[87,4,1024]{2,1,0:T(4,128)} %bitcast.4, f32[87,1024]{1,0:T(8,128)} %tgt_hbm.1, ...), custom_call_target="tpu_custom_call" | custom-call | tf_op jit(solution)/shard_map/crps_backward/pallas_call | solution.py:516
  52.5 2.1 %finish.1 = (bf16[4,512,1024]{2,1,0:T(8,128)(2,1)}, f32[16,512]{1,0:T(8,128)}, f32[16,87]{1,0:T(8,128)}, f32[1,16]{1,0:T(1,128)}) custom-call(bf16[4,512,1024]{2,1,0:T(8,128)(2,1)S(1)} %get-tuple-element.10.ig_ref, bf16[8,16,640]{2,1,0:T(8,128)(2,1)S(1)} %get-tuple-element.11.owned_ref), custom_call_target="tpu_custom_call" | custom-call | tf_op jit(solution)/shard_map/finish/pallas_call | solution.py:571
